TPU v7x, 32 devices: a whole 2x2x4 slice. The times are simulated.
32 devices in a mesh: seq: 2 (over x), shard: 16 (over z, y, core).
Axes of the slice: x: 2, y: 2, z: 4, core: 2. Of those that a mesh axis runs over, the one named last changes fastest.
Arguments:
- tokens: bfloat16 [16, 1024, 768], P('shard', 'seq'), may hold values from -6 to 6
- doc_lengths: int32 [16, 8], replicated, may hold values from 1 to 769, as said below
- qkv_weight: bfloat16 [768, 2304], P('shard'), may hold values from -0.21875 to 0.21875
- out_weight: bfloat16 [768, 768], P('shard'), may hold values from -2.5 to 2.5
- gate_weight: bfloat16 [768, 3072], P('shard'), may hold values from -0.21875 to 0.21875
- up_weight: bfloat16 [768, 3072], P('shard'), may hold values from -0.21875 to 0.21875
- down_weight: bfloat16 [3072, 768], P('shard'), may hold values from -0.109375 to 0.109375
- norm1_gain: bfloat16 [768], P('shard'), may hold values from 0.5 to 1.5
- norm1_bias: bfloat16 [768], P('shard'), may hold values from -3 to 3
- norm2_gain: bfloat16 [768], P('shard'), may hold values from 0.5 to 1.5
- norm2_bias: bfloat16 [768], P('shard'), may hold values from -3 to 3
- cotangent: bfloat16 [16, 1024, 768], P('shard', 'seq'), may hold values from -6 to 6
Outputs:
- layer_out: bfloat16 [16, 1024, 768], P('shard', 'seq')
- tokens_grad: float32 [16, 1024, 768], P('shard', 'seq')
- qkv_grad: float32 [768, 2304], P('shard')
- out_grad: float32 [768, 768], P('shard')
- gate_grad: float32 [768, 3072], P('shard')
- up_grad: float32 [768, 3072], P('shard')
- down_grad: float32 [3072, 768], P('shard')
- norm1_gain_grad: float32 [768], P('shard')
- norm1_bias_grad: float32 [768], P('shard')
- norm2_gain_grad: float32 [768], P('shard')
- norm2_bias_grad: float32 [768], P('shard')
Inputs may be any that keep to these rules, and one draw needn't show every extreme that they name: `doc_lengths`: each row sums to 1024; in every row one document has length 769 and begins within the first quarter of its sequence.
All inputs are finite; a program needn't handle non-finite values.
Results may differ from a plain program's by a relative error of at most 0.017.
Values may be sent and summed in bfloat16 or wider, within the bound.
No kernel may reach another device: no remote copies, remote signals or barrier semaphores. Data moves between devices by JAX's collectives and lax.ppermute only.
A program may use at most 192 MiB of HBM per device.

v0:
```python
from functools import partial

import jax
import jax.numpy as jnp
from jax import lax
from jax.sharding import PartitionSpec as P

D = 768
H = 12
HD = 64
HALF = 512


rope_base = 1000.0
norm_eps = 1e-05
big_negative = -1e30


def doc_layout(doc_sizes, length):
    doc_ends = jnp.cumsum(doc_sizes)
    doc_starts = doc_ends - doc_sizes
    places = jnp.arange(length, dtype=jnp.int32)
    segment = jnp.sum((places[:, None] >= doc_ends[None, :]).astype(jnp.int32), axis=1)
    onehot = segment[:, None] == jnp.arange(doc_sizes.shape[0], dtype=jnp.int32)[None, :]
    offset = jnp.sum(jnp.where(onehot, doc_starts[None, :], 0), axis=1)
    return (segment, places - offset)


def rotate(features, places, direction):
    half_dim = HD // 2
    frequency = rope_base ** (-jnp.arange(half_dim, dtype=jnp.float32) * 2.0 / HD)
    angles = places.astype(jnp.float32)[:, None] * frequency[None, :]
    cosine = jnp.cos(angles)[:, None, :]
    sine_part = direction * jnp.sin(angles)[:, None, :]
    lower_half = features[..., :half_dim]
    upper_half = features[..., half_dim:]
    return jnp.concatenate(
        [
            lower_half * cosine - upper_half * sine_part,
            upper_half * cosine + lower_half * sine_part,
        ],
        axis=-1,
    )


def normalize(residual, gain_vec, bias_vec):
    average = jnp.mean(residual, axis=-1, keepdims=True)
    centered = residual - average
    variance = jnp.mean(centered * centered, axis=-1, keepdims=True)
    return centered * lax.rsqrt(variance + norm_eps) * gain_vec + bias_vec


def swiglu(gate_pre, up_branch):
    return gate_pre / (1.0 + jnp.exp(-gate_pre)) * up_branch


def block_mask(segment, seg_pad, start):
    query_idx = start + jnp.arange(HALF, dtype=jnp.int32)
    key_idx = start - HALF + jnp.arange(3 * HALF, dtype=jnp.int32)
    seg_query = lax.dynamic_slice_in_dim(segment, start, HALF)
    seg_key = lax.dynamic_slice_in_dim(seg_pad, start, 3 * HALF)
    return (seg_query[:, None] == seg_key[None, :]) & (
        jnp.abs(query_idx[:, None] - key_idx[None, :]) <= HALF
    )


def masked_scores(mask, queries, keys_ctx):
    scores = jnp.einsum(
        "qd,kd->qk", queries, keys_ctx, preferred_element_type=jnp.float32
    ) * HD ** (-0.5)
    return jnp.where(mask, scores, big_negative)


def attend_head(segment, seg_pad, operands):
    queries, keys_pad, values_pad = operands
    seq_rows = queries.shape[0]

    def one_block(block):
        start = block * HALF
        query_blk = lax.dynamic_slice_in_dim(queries, start, HALF, 0)
        key_blk = lax.dynamic_slice_in_dim(keys_pad, start, 3 * HALF, 0)
        value_blk = lax.dynamic_slice_in_dim(values_pad, start, 3 * HALF, 0)
        scores = masked_scores(block_mask(segment, seg_pad, start), query_blk, key_blk)
        peak = jnp.max(scores, axis=1, keepdims=True)
        expo = jnp.exp(scores - peak)
        total = jnp.sum(expo, axis=1, keepdims=True)
        probs_low = (expo / total).astype(jnp.bfloat16)
        attended = jnp.dot(probs_low, value_blk, preferred_element_type=jnp.float32)
        return (attended.astype(jnp.bfloat16), (peak + jnp.log(total))[:, 0])

    attended, logsum = lax.map(one_block, jnp.arange(seq_rows // HALF, dtype=jnp.int32))
    return (attended.reshape(seq_rows, HD), logsum.reshape(seq_rows))


def attend_back(segment, seg_pad, operands):
    queries, keys_pad, values_pad, grad_att, logsum = operands
    seq_rows = queries.shape[0]

    def one_block(carry, block):
        grad_keys_pad, grad_values_pad = carry
        start = block * HALF
        query_blk = lax.dynamic_slice_in_dim(queries, start, HALF, 0)
        key_blk = lax.dynamic_slice_in_dim(keys_pad, start, 3 * HALF, 0)
        value_blk = lax.dynamic_slice_in_dim(values_pad, start, 3 * HALF, 0)
        grad_blk = lax.dynamic_slice_in_dim(grad_att, start, HALF, 0)
        logsum_blk = lax.dynamic_slice_in_dim(logsum, start, HALF, 0)
        scores = masked_scores(block_mask(segment, seg_pad, start), query_blk, key_blk)
        probs = jnp.exp(scores - logsum_blk[:, None])
        grad_probs = jnp.einsum(
            "qd,kd->qk", grad_blk, value_blk, preferred_element_type=jnp.float32
        )
        grad_values = jnp.einsum(
            "qk,qd->kd", probs.astype(jnp.bfloat16), grad_blk, preferred_element_type=jnp.float32
        )
        inner = jnp.sum(grad_probs * probs, axis=1, keepdims=True)
        grad_scores = (probs * (grad_probs - inner)).astype(jnp.bfloat16)
        grad_queries = jnp.dot(grad_scores, key_blk, preferred_element_type=jnp.float32) * HD ** (
            -0.5
        )
        grad_keys = jnp.einsum(
            "qk,qd->kd", grad_scores, query_blk, preferred_element_type=jnp.float32
        ) * HD ** (-0.5)
        old_keys = lax.dynamic_slice_in_dim(grad_keys_pad, start, 3 * HALF, 0)
        old_values = lax.dynamic_slice_in_dim(grad_values_pad, start, 3 * HALF, 0)
        grad_keys_pad = lax.dynamic_update_slice_in_dim(
            grad_keys_pad, old_keys + grad_keys, start, 0
        )
        grad_values_pad = lax.dynamic_update_slice_in_dim(
            grad_values_pad, old_values + grad_values, start, 0
        )
        return ((grad_keys_pad, grad_values_pad), grad_queries)

    empty = jnp.zeros((seq_rows + 2 * HALF, HD), jnp.float32)
    (grad_keys_pad, grad_values_pad), grad_queries = lax.scan(
        one_block, (empty, empty), jnp.arange(seq_rows // HALF, dtype=jnp.int32)
    )
    return (
        grad_queries.reshape(seq_rows, HD),
        grad_keys_pad[HALF : HALF + seq_rows],
        grad_values_pad[HALF : HALF + seq_rows],
    )


def head_major(block, rows, heads):
    return block.reshape(rows, heads, HD).transpose(1, 0, 2)


def token_major(block, rows, heads):
    return block.transpose(1, 0, 2).reshape(rows, heads * HD)


def local(
    tokens,
    doc_lengths,
    qkv_weight,
    out_weight,
    gate_weight,
    up_weight,
    down_weight,
    norm1_gain,
    norm1_bias,
    norm2_gain,
    norm2_bias,
    cotangent,
):
    groups = lax.axis_size("seq")
    seq_rank = lax.axis_index("seq")
    shard_rank = lax.axis_index("shard")
    tok_rows = tokens.shape[1]
    seq_rows = groups * tok_rows
    local_heads = H // groups
    local_width = local_heads * HD
    seq_row = lax.dynamic_slice_in_dim(doc_lengths, shard_rank, 1, 0)[0]
    segment, places = doc_layout(seq_row, seq_rows)
    own_places = lax.dynamic_slice_in_dim(places, seq_rank * tok_rows, tok_rows)
    rim_marks = jnp.full((HALF,), -1, jnp.int32)
    seg_pad = jnp.concatenate([rim_marks, segment, rim_marks])
    gathered = (
        lax.all_gather(qkv_weight, "shard", axis=0, tiled=True),
        lax.all_gather(out_weight, "shard", axis=0, tiled=True),
        lax.all_gather(gate_weight, "shard", axis=0, tiled=True),
        lax.all_gather(up_weight, "shard", axis=0, tiled=True),
        lax.all_gather(down_weight, "shard", axis=0, tiled=True),
        lax.all_gather(norm1_gain, "shard", axis=0, tiled=True),
        lax.all_gather(norm1_bias, "shard", axis=0, tiled=True),
        lax.all_gather(norm2_gain, "shard", axis=0, tiled=True),
        lax.all_gather(norm2_bias, "shard", axis=0, tiled=True),
    )
    wqkv_all, wout_all, wgate_all, wup_all, wdown_all, gain_one, bias_one, gain_two, bias_two = (
        gathered
    )
    gain_one = gain_one.astype(jnp.float32)
    bias_one = bias_one.astype(jnp.float32)
    gain_two = gain_two.astype(jnp.float32)
    bias_two = bias_two.astype(jnp.float32)
    rows_in = tokens[0]
    qkv = jnp.dot(rows_in, wqkv_all, preferred_element_type=jnp.float32)
    queries = rotate(qkv[:, :D].reshape(tok_rows, H, HD), own_places, 1.0).reshape(tok_rows, D)
    keys_rot = rotate(qkv[:, D : 2 * D].reshape(tok_rows, H, HD), own_places, 1.0).reshape(
        tok_rows, D
    )
    packed = jnp.stack([queries, keys_rot, qkv[:, 2 * D :]], axis=1).astype(jnp.bfloat16)
    heads = lax.all_to_all(packed, "seq", split_axis=2, concat_axis=0, tiled=True)
    query_heads = head_major(heads[:, 0], seq_rows, local_heads)
    key_pad = jnp.pad(
        head_major(heads[:, 1], seq_rows, local_heads), ((0, 0), (HALF, HALF), (0, 0))
    )
    value_pad = jnp.pad(
        head_major(heads[:, 2], seq_rows, local_heads), ((0, 0), (HALF, HALF), (0, 0))
    )
    attended, logsum = lax.map(
        partial(attend_head, segment, seg_pad), (query_heads, key_pad, value_pad)
    )
    merged = token_major(attended, seq_rows, local_heads)
    attn_tok = lax.all_to_all(merged, "seq", split_axis=0, concat_axis=1, tiled=True)
    branch = jnp.dot(attn_tok, wout_all, preferred_element_type=jnp.float32)
    normed_one, norm_one_back = jax.vjp(
        normalize, rows_in.astype(jnp.float32) + branch, gain_one, bias_one
    )
    first_low = normed_one.astype(jnp.bfloat16)
    gate_pre = jnp.dot(first_low, wgate_all, preferred_element_type=jnp.float32)
    up_branch = jnp.dot(first_low, wup_all, preferred_element_type=jnp.float32)
    hidden_f, swiglu_back = jax.vjp(swiglu, gate_pre, up_branch)
    hidden_low = hidden_f.astype(jnp.bfloat16)
    mlp_out = jnp.dot(hidden_low, wdown_all, preferred_element_type=jnp.float32)
    result_f, norm_two_back = jax.vjp(normalize, normed_one + mlp_out, gain_two, bias_two)
    layer_out = result_f.astype(jnp.bfloat16)[None]
    matrices = (
        lax.all_gather(qkv_weight, "shard", axis=0, tiled=True),
        lax.all_gather(out_weight, "shard", axis=0, tiled=True),
        lax.all_gather(gate_weight, "shard", axis=0, tiled=True),
        lax.all_gather(up_weight, "shard", axis=0, tiled=True),
        lax.all_gather(down_weight, "shard", axis=0, tiled=True),
    )
    back_qkv, back_out, back_gate, back_up, back_down = matrices
    grad_res_two, grad_gain_two, grad_bias_two = norm_two_back(cotangent[0].astype(jnp.float32))
    grad_mlp = grad_res_two.astype(jnp.bfloat16)
    grad_down = jnp.einsum("tf,td->fd", hidden_low, grad_mlp, preferred_element_type=jnp.float32)
    grad_hidden = jnp.einsum("td,fd->tf", grad_mlp, back_down, preferred_element_type=jnp.float32)
    grad_gate_f, grad_up_f = swiglu_back(grad_hidden)
    gate_low = grad_gate_f.astype(jnp.bfloat16)
    up_low = grad_up_f.astype(jnp.bfloat16)
    grad_wgate = jnp.einsum("td,tf->df", first_low, gate_low, preferred_element_type=jnp.float32)
    grad_wup = jnp.einsum("td,tf->df", first_low, up_low, preferred_element_type=jnp.float32)
    grad_normed = grad_res_two + jnp.einsum(
        "tf,df->td", gate_low, back_gate, preferred_element_type=jnp.float32
    )
    grad_normed = grad_normed + jnp.einsum(
        "tf,df->td", up_low, back_up, preferred_element_type=jnp.float32
    )
    grad_res_one, grad_gain_one, grad_bias_one = norm_one_back(grad_normed)
    branch_low = grad_res_one.astype(jnp.bfloat16)
    grad_wout = jnp.einsum("td,te->de", attn_tok, branch_low, preferred_element_type=jnp.float32)
    grad_attn = jnp.einsum(
        "te,de->td", branch_low, back_out, preferred_element_type=jnp.float32
    ).astype(jnp.bfloat16)
    grad_heads = lax.all_to_all(grad_attn, "seq", split_axis=1, concat_axis=0, tiled=True)
    grad_att_heads = head_major(grad_heads, seq_rows, local_heads)
    grad_q, grad_k, grad_v = lax.map(
        partial(attend_back, segment, seg_pad),
        (query_heads, key_pad, value_pad, grad_att_heads, logsum),
    )
    grad_q_rot = rotate(grad_q.transpose(1, 0, 2), places, -1.0).reshape(seq_rows, local_width)
    grad_k_rot = rotate(grad_k.transpose(1, 0, 2), places, -1.0).reshape(seq_rows, local_width)
    grad_pack = jnp.stack(
        [grad_q_rot, grad_k_rot, token_major(grad_v, seq_rows, local_heads)], axis=1
    ).astype(jnp.bfloat16)
    grad_qkv = lax.all_to_all(grad_pack, "seq", split_axis=0, concat_axis=2, tiled=True).reshape(
        tok_rows, 3 * D
    )
    grad_wqkv = jnp.einsum("td,te->de", rows_in, grad_qkv, preferred_element_type=jnp.float32)
    grad_in = grad_res_one + jnp.einsum(
        "te,de->td", grad_qkv, back_qkv, preferred_element_type=jnp.float32
    )
    grad_terms = (
        grad_wqkv,
        grad_wout,
        grad_wgate,
        grad_wup,
        grad_down,
        grad_gain_one,
        grad_bias_one,
        grad_gain_two,
        grad_bias_two,
    )
    pieces = (
        lax.psum_scatter(grad_terms[0], "shard", scatter_dimension=0, tiled=True),
        lax.psum_scatter(grad_terms[1], "shard", scatter_dimension=0, tiled=True),
        lax.psum_scatter(grad_terms[2], "shard", scatter_dimension=0, tiled=True),
        lax.psum_scatter(grad_terms[3], "shard", scatter_dimension=0, tiled=True),
        lax.psum_scatter(grad_terms[4], "shard", scatter_dimension=0, tiled=True),
        lax.psum_scatter(grad_terms[5], "shard", scatter_dimension=0, tiled=True),
        lax.psum_scatter(grad_terms[6], "shard", scatter_dimension=0, tiled=True),
        lax.psum_scatter(grad_terms[7], "shard", scatter_dimension=0, tiled=True),
        lax.psum_scatter(grad_terms[8], "shard", scatter_dimension=0, tiled=True),
    )
    owned = (
        lax.psum(pieces[0].astype(jnp.bfloat16), "seq").astype(jnp.float32),
        lax.psum(pieces[1].astype(jnp.bfloat16), "seq").astype(jnp.float32),
        lax.psum(pieces[2].astype(jnp.bfloat16), "seq").astype(jnp.float32),
        lax.psum(pieces[3].astype(jnp.bfloat16), "seq").astype(jnp.float32),
        lax.psum(pieces[4].astype(jnp.bfloat16), "seq").astype(jnp.float32),
        lax.psum(pieces[5].astype(jnp.bfloat16), "seq").astype(jnp.float32),
        lax.psum(pieces[6].astype(jnp.bfloat16), "seq").astype(jnp.float32),
        lax.psum(pieces[7].astype(jnp.bfloat16), "seq").astype(jnp.float32),
        lax.psum(pieces[8].astype(jnp.bfloat16), "seq").astype(jnp.float32),
    )
    return (
        layer_out,
        grad_in[None],
        owned[0],
        owned[1],
        owned[2],
        owned[3],
        owned[4],
        owned[5],
        owned[6],
        owned[7],
        owned[8],
    )


def solution(mesh):
    placed = (
        P("shard", "seq", None),
        P(),
        P("shard", None),
        P("shard", None),
        P("shard", None),
        P("shard", None),
        P("shard", None),
        P("shard"),
        P("shard"),
        P("shard"),
        P("shard"),
        P("shard", "seq", None),
    )
    return jax.shard_map(
        local,
        mesh=mesh,
        in_specs=placed,
        out_specs=(
            P("shard", "seq", None),
            P("shard", "seq", None),
            P("shard", None),
            P("shard", None),
            P("shard", None),
            P("shard", None),
            P("shard", None),
            P("shard"),
            P("shard"),
            P("shard"),
            P("shard"),
        ),
        check_vma=False,
    )
```

profile of v0, /device:TPU:0, one launch (start us, length us, event | category | flops | bytes accessed | tf_op | source)
XLA Modules:
  0.0 1009.1 jit_solution(825504227507533848)
XLA Ops:
  11.5 48.7 %all-gather.6.cloned.1.call-done = bf16[768,2304]{1,0:T(8,128)(2,1)} async-done(((bf16[48,2304]{1,0:T(8,128)(2,1)}), bf16[768,2304]{1,0:T(8,128)(2,1)}) %all-gather.6.cloned.1.call-update) | async-done | bytes 3538960 | tf_op jit(solution)/shard_map/all_gather | solution.py:179
  60.2 4.2 fusion.45
  73.5 4.3 copy.178
  77.8 5.2 all-to-all-start
  83.7 36.2 %all-to-all-done = bf16[512,3,768]{0,1,2:T(4,128)(2,1)} async-done(((bf16[512,3,768]{0,1,2:T(4,128)(2,1)}), bf16[512,3,768]{0,1,2:T(4,128)(2,1)}, u32[]{:S(2)}, u32[]{:S(2)}) %all-to-all-start) | async-done | bytes 2359328 | tf_op jit(solution)/shard_map/all_to_all | solution.py:203
  119.9 3.9 copy.179
  123.7 3.0 copy.180
  139.8 69.9 %while.84 = (s32[]{:T(128)}, bf16[6,1024,64]{2,1,0:T(8,128)(2,1)}, f32[6,1024]{1,0:T(8,128)S(1)}, bf16[6,1024,64]{2,1,0:T(8,128)(2,1)}, bf16[6,2048,64]{2,1,0:T(...) while((s32[]{:T(128)}, bf16[6,1024,64]{2,1,0:T(8,128)(2,1)}, ...), condition=%wide.region_8.9_spmd, body=%wide.region_3.8_spmd.sunk | while | flops 211584512 | bytes 12468813 | solution.py:211
  142.1 8.3 while.87
  153.8 8.3 while.87
  165.4 8.3 while.87
  177.1 8.3 while.87
  188.7 8.3 while.87
  200.4 8.3 while.87
  213.0 3.5 all-to-all-start.1
  218.8 32.5 %all-reduce.11 = (bf16[768]{0:T(1024)(128)(2,1)S(1)}, bf16[768]{0:T(1024)(128)(2,1)S(1)}, bf16[768]{0:T(1024)(128)(2,1)S(1)}, bf16[768]{0:T(1024)(128)(2,1)S(1)}) all-reduce(bf16[768]{0:T(1024)(128)(2,1)S(1)} %dynamic-update-slice.1, bf16[768]{0:T(1024)(128)(2,1)S(1)} %dynamic-update-slice, ...), channel_id=1, replica_groups=mesh['seq'=2,'shard'=16] {'shard'}, use_global_device_ids=true, to_apply=%add.3 | all-reduce | flops 3072 | bytes 12288
  251.4 2.5 fusion.61
  254.5 7.2 fusion.63
  261.7 9.2 multiply_convert_fusion.2
  270.9 6.0 fusion.62
  281.0 9.7 multiply_convert_fusion.1
  290.8 2.7 fusion.64
  293.5 6.2 multiply_reduce_fusion.1
  303.0 3.5 all-to-all-start.2
  310.3 6.3 all-to-all-done.2
  318.8 101.9 %while.86 = (s32[]{:T(128)}, f32[6,1024,64]{1,2,0:T(8,128)}, f32[6,1024,64]{1,2,0:T(8,128)}, bf16[6,1024,64]{1,2,0:T(8,128)(2,1)}, bf16[6,1024,64]{2,1,0:T(8,128...) while((s32[]{:T(128)}, f32[6,1024,64]{1,2,0:T(8,128)}, ...), condition=%wide.region_21.22_spmd, body=%wide.region_17.21_spmd.sunk | while | flops 514655744 | bytes 32307912 | solution.py:259
  322.6 10.9 %while.88 = (s32[]{:T(128)}, f32[2048,64]{0,1:T(8,128)S(1)}, f32[2048,64]{0,1:T(8,128)S(1)}, f32[2,512,64]{1,2,0:T(8,128)S(1)}, s32[2]{0:T(128)S(1)}, /*index=5*...) while((s32[]{:T(128)}, f32[2048,64]{0,1:T(8,128)S(1)}, ...), condition=%wide.region_20.20_spmd, body=%wide.region_18.19_spmd.sunk | while | flops 514655744 | bytes 27056456 | solution.py:134
  339.6 10.9 %while.88 = (s32[]{:T(128)}, f32[2048,64]{0,1:T(8,128)S(1)}, f32[2048,64]{0,1:T(8,128)S(1)}, f32[2,512,64]{1,2,0:T(8,128)S(1)}, s32[2]{0:T(128)S(1)}, /*index=5*...) while((s32[]{:T(128)}, f32[2048,64]{0,1:T(8,128)S(1)}, ...), condition=%wide.region_20.20_spmd, body=%wide.region_18.19_spmd.sunk | while | flops 514655744 | bytes 27056456 | solution.py:134
  356.5 10.9 %while.88 = (s32[]{:T(128)}, f32[2048,64]{0,1:T(8,128)S(1)}, f32[2048,64]{0,1:T(8,128)S(1)}, f32[2,512,64]{1,2,0:T(8,128)S(1)}, s32[2]{0:T(128)S(1)}, /*index=5*...) while((s32[]{:T(128)}, f32[2048,64]{0,1:T(8,128)S(1)}, ...), condition=%wide.region_20.20_spmd, body=%wide.region_18.19_spmd.sunk | while | flops 514655744 | bytes 27056456 | solution.py:134
  373.4 10.9 %while.88 = (s32[]{:T(128)}, f32[2048,64]{0,1:T(8,128)S(1)}, f32[2048,64]{0,1:T(8,128)S(1)}, f32[2,512,64]{1,2,0:T(8,128)S(1)}, s32[2]{0:T(128)S(1)}, /*index=5*...) while((s32[]{:T(128)}, f32[2048,64]{0,1:T(8,128)S(1)}, ...), condition=%wide.region_20.20_spmd, body=%wide.region_18.19_spmd.sunk | while | flops 514655744 | bytes 27056456 | solution.py:134
  390.4 10.9 %while.88 = (s32[]{:T(128)}, f32[2048,64]{0,1:T(8,128)S(1)}, f32[2048,64]{0,1:T(8,128)S(1)}, f32[2,512,64]{1,2,0:T(8,128)S(1)}, s32[2]{0:T(128)S(1)}, /*index=5*...) while((s32[]{:T(128)}, f32[2048,64]{0,1:T(8,128)S(1)}, ...), condition=%wide.region_20.20_spmd, body=%wide.region_18.19_spmd.sunk | while | flops 514655744 | bytes 27056456 | solution.py:134
  407.2 10.9 %while.88 = (s32[]{:T(128)}, f32[2048,64]{0,1:T(8,128)S(1)}, f32[2048,64]{0,1:T(8,128)S(1)}, f32[2,512,64]{1,2,0:T(8,128)S(1)}, s32[2]{0:T(128)S(1)}, /*index=5*...) while((s32[]{:T(128)}, f32[2048,64]{0,1:T(8,128)S(1)}, ...), condition=%wide.region_20.20_spmd, body=%wide.region_18.19_spmd.sunk | while | flops 514655744 | bytes 27056456 | solution.py:134
  420.7 2.3 subtract_convert_fusion.1
  425.9 4.9 copy.198
  430.7 37.0 %all_to_all.68 = bf16[1024,3,384]{2,1,0:T(4,128)(2,1)S(1)} all-to-all(bf16[1024,3,384]{2,1,0:T(4,128)(2,1)S(1)} %copy.198), channel_id=1, replica_groups=mesh['seq'=2,'shard'=16] {'seq'}, dimensions={0} | all-to-all | bytes 4718592 | tf_op jit(solution)/shard_map/all_to_all | solution.py:268
  469.5 2.9 copy.200
  472.4 4.9 convolution_bitcast_fusion
  477.3 8.0 copy.203
  486.4 7.2 fusion.65
  493.8 7.5 fusion.66
  502.0 9.2 fusion.52
  512.8 60.7 %reduce-scatter.16.cloned.1.call-done = f32[48,2304]{1,0:T(8,128)} async-done(((f32[768,2304]{1,0:T(8,128)}), f32[48,2304]{1,0:T(8,128)}) %reduce-scatter.16.cloned.1.call-update) | async-done | bytes 442384
  575.5 112.9 %reduce-scatter.10.cloned.1.call-done = f32[48,3072]{1,0:T(8,128)} async-done(((f32[768,3072]{1,0:T(8,128)}), f32[48,3072]{1,0:T(8,128)}) %reduce-scatter.10.cloned.1.call-update) | async-done | bytes 589840 | tf_op jit(solution)/shard_map/reduce_scatter | solution.py:289
  690.2 114.0 %reduce-scatter.12.cloned.1.call-done = f32[48,3072]{1,0:T(8,128)} async-done(((f32[768,3072]{1,0:T(8,128)}), f32[48,3072]{1,0:T(8,128)}) %reduce-scatter.12.cloned.1.call-update) | async-done | bytes 589840 | tf_op jit(solution)/shard_map/reduce_scatter | solution.py:290
  806.0 113.2 %reduce-scatter.14.cloned.1.call-done = f32[192,768]{1,0:T(8,128)} async-done(((f32[3072,768]{1,0:T(8,128)}), f32[192,768]{1,0:T(8,128)}) %reduce-scatter.14.cloned.1.call-update) | async-done | bytes 589840 | tf_op jit(solution)/shard_map/reduce_scatter | solution.py:291
  921.9 60.2 %all-reduce.10 = (bf16[768]{0:T(1024)(128)(2,1)S(1)}, bf16[768]{0:T(1024)(128)(2,1)S(1)}, bf16[768]{0:T(1024)(128)(2,1)S(1)}, bf16[768]{0:T(1024)(128)(2,1)S(1)}) all-reduce(f32[768]{0:T(1024)S(1)} %copy-done.27, f32[768]{0:T(1024)S(1)} %copy-done.28, f32[768]{0:T(1024)S(1)} %copy-done.24, ...), channel_id=7, replica_groups=mesh['seq'=2,'shard'=16] {'shard'}, use_global_device_ids=true, to_apply=%region_33.34.clone | all-reduce | flops 3072 | bytes 18432
  982.5 4.9 all-reduce.12
  989.4 5.7 add_bitcast_fusion
  (608 shorter events, 224.6 us)
Async XLA Ops:
  7.2 2.8 copy-start
  7.2 53.0 %all-gather.6.cloned.1.call-start = ((), (), s32[]{:S(2)}) async-start(), calls=%async_computation.9 | async-start | bytes 3760128 | tf_op jit(solution)/shard_map/all_gather | solution.py:179
  7.9 243.4 %all-gather.8.cloned.1.call-start = ((), (), s32[]{:S(2)}) async-start(), calls=%async_computation.10 | async-start | bytes 1253376 | tf_op jit(solution)/shard_map/all_gather | solution.py:180
  8.7 245.8 %all-gather.10.cloned.1.call-start = ((), (), s32[]{:S(2)}) async-start(), calls=%async_computation.11 | async-start | bytes 5013504 | tf_op jit(solution)/shard_map/all_gather | solution.py:181
  9.4 252.3 %all-gather.12.cloned.1.call-start = ((), (), s32[]{:S(2)}) async-start(), calls=%async_computation.12 | async-start | bytes 5013504 | tf_op jit(solution)/shard_map/all_gather | solution.py:182
  64.5 2.7 copy-start.8
  71.7 1.6 copy-start.10
  77.8 42.0 %all-to-all-start = ((bf16[512,3,768]{0,1,2:T(4,128)(2,1)}), bf16[512,3,768]{0,1,2:T(4,128)(2,1)}, u32[]{:S(2)}, u32[]{:S(2)}) async-start(bf16[512,3,768]{0,1,2:T(4,128)(2,1)} %copy.178), calls=%async_computation | async-start | bytes 6291456 | tf_op jit(solution)/shard_map/all_to_all | solution.py:203
  83.0 187.9 %all-gather.14.cloned.1.call-start = ((), (), s32[]{:S(2)}) async-start(), calls=%async_computation.13 | async-start | bytes 5013504 | tf_op jit(solution)/shard_map/all_gather | solution.py:183
  212.0 4.6 copy-start.31
  212.0 5.8 copy-start.35
  212.0 6.1 copy-start.36
  212.0 6.3 copy-start.37
  212.0 6.5 copy-start.38
  212.0 39.3 %copy-start.17 = (bf16[1,512,768]{2,1,0:T(8,128)(2,1)S(1)}, bf16[1,512,768]{2,1,0:T(8,128)(2,1)}, u32[]{:S(2)}) copy-start(bf16[1,512,768]{2,1,0:T(8,128)(2,1)} %param.20) | copy-start | bytes 2359300
  213.0 38.3 %all-to-all-start.1 = ((bf16[2,512,384]{1,2,0:T(8,128)(2,1)}), bf16[2,512,384]{1,2,0:T(8,128)(2,1)S(1)}, u32[]{:S(2)}, u32[]{:S(2)}) async-start(bf16[2,512,384]{1,2,0:T(8,128)(2,1)} %copy.188), calls=%async_computation.1 | async-start | bytes 1572864 | tf_op jit(solution)/shard_map/all_to_all | solution.py:215
  251.3 2.5 copy-start.13
  254.5 7.2 copy-start.2
  278.1 2.9 copy-start.6
  279.4 11.4 %slice-start = ((s8[4718592]{0:T(1024)(128)(4,1)}), s8[4194304]{0:T(1024)(128)(4,1)S(1)}, s32[]{:S(2)}) async-start(s8[4718592]{0:T(1024)(128)(4,1)} %bitcast.192), calls=%async_computation.20 | async-start | bytes 8388608
  281.0 12.5 %copy-start.15 = (f32[512,768]{1,0:T(8,128)}, f32[512,768]{1,0:T(8,128)S(1)}, u32[]{:S(2)}) copy-start(f32[512,768]{1,0:T(8,128)S(1)} %get-tuple-element.871) | copy-start | bytes 4718596
  281.0 12.5 %copy-start.32 = (f32[512]{0:T(512)}, f32[512]{0:T(512)S(1)}, u32[]{:S(2)}) copy-start(f32[512]{0:T(512)S(1)} %negate_multiply_fusion.1) | copy-start | bytes 6148
  281.0 9.8 slice-start.1
  290.7 2.7 copy-start.12
  290.7 2.7 copy-start.11
  300.3 7.5 copy-start.7
  300.4 7.5 copy-start.25
  301.8 4.8 copy-start.23
  301.8 4.8 copy-start.30
  301.8 6.0 copy-start.14
  303.0 13.6 %all-to-all-start.2 = ((bf16[512,2,384]{0,2,1:T(8,128)(2,1)}), bf16[512,2,384]{0,2,1:T(8,128)(2,1)S(1)}, u32[]{:S(2)}, u32[]{:S(2)}) async-start(bf16[512,2,384]{0,2,1:T(8,128)(2,1)} %bitcast.43), calls=%async_computation.2 | async-start | bytes 1572864 | tf_op jit(solution)/shard_map/all_to_all | solution.py:257
  306.5 204.7 %reduce-scatter.8.cloned.1.call-start = ((), (), s32[]{:S(2)}) async-start(), calls=%async_computation.14 | async-start | bytes 2506752 | tf_op jit(solution)/shard_map/reduce_scatter | solution.py:288
  310.2 263.3 %reduce-scatter.16.cloned.1.call-start = ((), (), s32[]{:S(2)}) async-start(), calls=%async_computation.18 | async-start | bytes 7520256
  318.8 101.9 %copy-start.19 = (f32[1024,32]{0,1:T(8,128)S(1)}, f32[1024,32]{0,1:T(8,128)}, u32[]{:S(2)}) copy-start(f32[1024,32]{0,1:T(8,128)} %get-tuple-element.900) | copy-start | bytes 393220
  318.8 101.9 %copy-start.20 = (f32[1024,32]{0,1:T(8,128)S(1)}, f32[1024,32]{0,1:T(8,128)}, u32[]{:S(2)}) copy-start(f32[1024,32]{0,1:T(8,128)} %get-tuple-element.901) | copy-start | bytes 393220
  469.5 2.9 copy-start.18
  485.3 203.1 %reduce-scatter.10.cloned.1.call-start = ((), (), s32[]{:S(2)}) async-start(), calls=%async_computation.15 | async-start | bytes 10027008 | tf_op jit(solution)/shard_map/reduce_scatter | solution.py:289
  493.7 310.5 %reduce-scatter.12.cloned.1.call-start = ((), (), s32[]{:S(2)}) async-start(), calls=%async_computation.16 | async-start | bytes 10027008 | tf_op jit(solution)/shard_map/reduce_scatter | solution.py:290
  501.3 418.0 %reduce-scatter.14.cloned.1.call-start = ((), (), s32[]{:S(2)}) async-start(), calls=%async_computation.17 | async-start | bytes 10027008 | tf_op jit(solution)/shard_map/reduce_scatter | solution.py:291
  511.2 484.0 %all-reduce.16.cloned.1.call-start = ((), (), s32[]{:S(2)}) async-start(), calls=%async_computation.19 | async-start | bytes 3096576 | tf_op jit(solution)/shard_map/psum | solution.py:298
  690.2 231.5 %copy-start.5 = (bf16[1,512,768]{2,1,0:T(8,128)(2,1)S(1)}, bf16[1,512,768]{2,1,0:T(8,128)(2,1)}, u32[]{:S(2)}) copy-start(bf16[1,512,768]{2,1,0:T(8,128)(2,1)} %param.31) | copy-start | bytes 2359300
  806.0 115.9 %copy-start.24 = (f32[768]{0:T(1024)S(1)}, f32[768]{0:T(1024)}, u32[]{:S(2)}) copy-start(f32[768]{0:T(1024)} %get-tuple-element.768) | copy-start | bytes 9220
  806.0 115.9 %copy-start.27 = (f32[768]{0:T(1024)S(1)}, f32[768]{0:T(1024)}, u32[]{:S(2)}) copy-start(f32[768]{0:T(1024)} %get-tuple-element.766) | copy-start | bytes 9220
  806.0 115.9 %copy-start.28 = (f32[768]{0:T(1024)S(1)}, f32[768]{0:T(1024)}, u32[]{:S(2)}) copy-start(f32[768]{0:T(1024)} %get-tuple-element.770) | copy-start | bytes 9220
  806.0 183.4 %copy-start.26 = (f32[512]{0:T(512)S(1)}, f32[512]{0:T(512)}, u32[]{:S(2)}) copy-start(f32[512]{0:T(512)} %copy-done.25) | copy-start | bytes 6148
  995.1 5.5 copy-start.22
  995.1 6.3 copy-start.21
  995.1 7.2 copy-start.1
  (7 other events, 7.8 us)
Sparse Core Ops, SparseCore 0:
  10.3 49.8 all-gather.5
  62.5 37.3 all-gather.7
  102.2 52.2 all-gather.9
  156.7 51.7 all-gather.11
  210.6 52.3 all-gather.13
  310.8 60.8 reduce-scatter.7
  485.5 87.9 reduce-scatter.15
  577.6 110.8 reduce-scatter.9
  693.1 111.0 reduce-scatter.11
  808.2 111.0 reduce-scatter.13
  922.7 51.4 all-reduce.15
where the time goes:
time: 1020 us; the launch traced here: 1010 us
  waiting for transfers between devices  495 us (49%)
  matrix products  154 us (15%)
  local copies, waits for them, and re-layouts  141 us (14%)
  blocking collectives  135 us (13%)
  other arithmetic  37.7 us (4%)
  loops' own time  17.9 us (2%)
  between operations  16.2 us (2%)
  starting transfers between devices  13.3 us (1%)
    reduce_scatter x1, waiting for transfers between devices, local(): lax.psum_scatter(grad_terms[3], 'shard', scatter_dimension=0, tiled=True)  114 us
    reduce_scatter x1, waiting for transfers between devices, local(): lax.psum_scatter(grad_terms[4], 'shard', scatter_dimension=0, tiled=True)  113 us
    reduce_scatter x1, waiting for transfers between devices, local(): lax.psum_scatter(grad_terms[2], 'shard', scatter_dimension=0, tiled=True)  113 us
    unnamed x2, blocking collectives  92.7 us
    unnamed x12, waiting for transfers between devices  63.6 us
    all_gather x1, waiting for transfers between devices, local(): lax.all_gather(qkv_weight, 'shard', axis=0, tiled=True)  48.7 us
    all_to_all x1, blocking collectives, local(): lax.all_to_all(grad_pack, 'seq', split_axis=0, concat_axis=2, tiled=True)  37 us
    all_to_all x1, waiting for transfers between devices, local(): lax.all_to_all(packed, 'seq', split_axis=2, concat_axis=0, tiled=True)  36.2 us
  transfers between devices with their start and end apart: 14, of which 7 were waited for; matrix products, arithmetic and copies ran while one was open for 28% of the time, Pallas kernels for 0%

commit v1 on v0

v1 whole, which is shorter than its diff:
```python
from functools import partial

import jax
import jax.numpy as jnp
from jax import lax
from jax.experimental import pallas as pl
from jax.experimental.pallas import tpu as pltpu
from jax.sharding import PartitionSpec as P

D = 768
H = 12
HD = 64
FF = 3072
HALF = 512
PAIRS = H // 2
BLK = 768
MIB = 1 << 20

rope_base = 1000.0
norm_eps = 1e-05
big_negative = -1e30

bf16 = jnp.bfloat16
f32 = jnp.float32
VM = pl.BlockSpec(memory_space=pltpu.VMEM)
SM = pl.BlockSpec(memory_space=pltpu.SMEM)
HBM = pl.BlockSpec(memory_space=pl.ANY)


def dot(a, b):
    return lax.dot_general(a, b, (((1,), (0,)), ((), ())), preferred_element_type=f32)


def dot_t(a, b):
    return lax.dot_general(a, b, (((1,), (1,)), ((), ())), preferred_element_type=f32)


def params(mib):
    return pltpu.CompilerParams(vmem_limit_bytes=mib * MIB)


def cost(flops, moved, trans=0):
    return pl.CostEstimate(flops=int(flops), bytes_accessed=int(moved), transcendentals=int(trans))


def shape(dims, kind):
    return jax.ShapeDtypeStruct(dims, kind)


def piece_copies(meta, pieces, dst, sems):
    x, z, y, c = meta[0], meta[1], meta[2], meta[3]
    rows = pieces[0].shape[1]
    copies = []
    for at, piece in enumerate(pieces):
        dc, dy, dh = at // 4, (at // 2) % 2, at % 2
        h = jnp.where(x == 0, dh, 1 - dh)
        yy = jnp.where(y == 0, dy, 1 - dy)
        cc = jnp.where(c == 0, dc, 1 - dc)
        for k in range(4):
            zz = lax.rem(z - k + 4, 4)
            row = pl.multiple_of(((zz * 2 + yy) * 2 + cc) * rows, rows)
            copies.append(
                pltpu.make_async_copy(
                    piece.at[k], dst.at[h, pl.ds(row, rows)], sems.at[at * 4 + k]
                )
            )
    return copies


def spin(u, cosine, sine):
    lane = lax.broadcasted_iota(jnp.int32, u.shape, 1)
    swapped = jnp.where(lane % HD < HD // 2, pltpu.roll(u, 96, 1), pltpu.roll(u, 32, 1))
    return u * cosine + swapped * sine


def qkv_kernel(meta, own, other, cosine, sine, *rest):
    pieces = rest[:8]
    q_out, k_out, kt_out, v_out, vt_out, w_out, w, sems, out_sem = rest[8:]
    step = pl.program_id(0)
    copies = piece_copies(meta, pieces, w, sems)

    @pl.when(step == 0)
    def _():
        for copy in copies:
            copy.start()
        for copy in copies:
            copy.wait()
        pltpu.make_async_copy(w, w_out, out_sem).start()

    col = pl.multiple_of(step * 256, 256)
    wq = w[0, :, pl.ds(col, 256)]
    wk = w[0, :, pl.ds(pl.multiple_of(col + D, 256), 256)]
    wv = w[1, :, pl.ds(col, 256)]
    for half, rows in enumerate((own, other)):
        at = slice(half * HALF, (half + 1) * HALF)
        xs = rows[...]
        cs, sn = cosine[at, :], sine[at, :]
        qs, ks, vs = dot(xs, wq), dot(xs, wk), dot(xs, wv).astype(bf16)
        for i in range(2):
            lanes = slice(i * 128, (i + 1) * 128)
            q_out[at, lanes] = spin(qs[:, lanes], cs, sn).astype(bf16)
            kr = spin(ks[:, lanes], cs, sn).astype(bf16)
            k_out[at, lanes] = kr
            kt_out[lanes, at] = kr.T
        v_out[at, :] = vs
        vt_out[:, at] = vs.T

    @pl.when(step == 2)
    def _():
        pltpu.make_async_copy(w, w_out, out_sem).wait()


def qkv_call(meta, own, other, cosine, sine, pieces):
    rows = 2 * HALF
    full = pl.BlockSpec((rows, 128), lambda i: (0, 0))
    x_spec = pl.BlockSpec((HALF, D), lambda i: (0, 0))
    nat = pl.BlockSpec((rows, 256), lambda i: (0, i))
    tr = pl.BlockSpec((256, rows), lambda i: (i, 0))
    return pl.pallas_call(
        qkv_kernel,
        grid=(3,),
        in_specs=[SM, x_spec, x_spec, full, full] + [HBM] * 8,
        out_specs=[nat, nat, tr, nat, tr, HBM],
        out_shape=[
            shape((rows, D), bf16),
            shape((rows, D), bf16),
            shape((D, rows), bf16),
            shape((rows, D), bf16),
            shape((D, rows), bf16),
            shape((2, D, 2 * BLK), bf16),
        ],
        scratch_shapes=[
            pltpu.VMEM((2, D, 2 * BLK), bf16),
            pltpu.SemaphoreType.DMA((32,)),
            pltpu.SemaphoreType.DMA,
        ],
        compiler_params=params(48),
        cost_estimate=cost(2 * rows * D * 3 * D, 20e6),
        name="qkv",
    )(meta, own, other, cosine, sine, *pieces)


def segment_of(meta, pos):
    seg = jnp.zeros(pos.shape, jnp.int32)
    for d in range(8):
        seg = seg + jnp.where(pos >= meta[8 + d], 1, 0)
    return seg


def bias_of(meta, key_base, keys, query_base):
    row = lax.broadcasted_iota(jnp.int32, (keys, 128), 0)
    key_pos = jnp.where(row < HALF, row + key_base[0], row - HALF + key_base[1])
    key_seg = segment_of(meta, key_pos)[:, :1]
    key_pos = key_pos[:, :1]
    query_pos = lax.broadcasted_iota(jnp.int32, (8, HALF), 1) + query_base
    query_seg = segment_of(meta, query_pos)[:1]
    query_pos = query_pos[:1]
    near = jnp.abs(key_pos - query_pos) <= HALF
    return jnp.where((key_seg == query_seg) & near, 0.0, big_negative).astype(f32)


def head_part(block, hh, scale=None):
    lane = lax.broadcasted_iota(jnp.int32, block.shape, 1)
    kept = jnp.where((lane // HD) == hh, block, jnp.zeros_like(block))
    return kept if scale is None else kept * jnp.asarray(scale, block.dtype)


def attend_kernel(meta, q, k, vt, att, att_t, lse, bias):
    @pl.when(pl.program_id(0) == 0)
    def _():
        own, other = meta[0] * HALF, HALF - meta[0] * HALF
        bias[...] = bias_of(meta, (own, other), 2 * HALF, own)

    parts = []
    for hh in range(2):
        qz = head_part(q[...], hh, HD**-0.5)
        s = dot_t(k[...], qz) + bias[...]
        peak = jnp.max(s, axis=0, keepdims=True)
        e = jnp.exp(s - peak)
        total = jnp.sum(e, axis=0, keepdims=True)
        o = dot(vt[hh * HD : (hh + 1) * HD, :], e.astype(bf16)) * (1.0 / total)
        parts.append(o.astype(bf16))
        lse[0, hh : hh + 1, :] = peak + jnp.log(total)
    both = jnp.concatenate(parts, axis=0)
    att_t[...] = both
    att[...] = both.T


def attend_call(meta, q, k, vt):
    return pl.pallas_call(
        attend_kernel,
        grid=(PAIRS,),
        in_specs=[
            SM,
            pl.BlockSpec((HALF, 128), lambda i: (0, i)),
            pl.BlockSpec((2 * HALF, 128), lambda i: (0, i)),
            pl.BlockSpec((128, 2 * HALF), lambda i: (i, 0)),
        ],
        out_specs=[
            pl.BlockSpec((HALF, 128), lambda i: (0, i)),
            pl.BlockSpec((128, HALF), lambda i: (i, 0)),
            pl.BlockSpec((1, 2, HALF), lambda i: (i, 0, 0)),
        ],
        out_shape=[
            shape((HALF, D), bf16),
            shape((D, HALF), bf16),
            shape((PAIRS, 2, HALF), f32),
        ],
        scratch_shapes=[pltpu.VMEM((2 * HALF, HALF), f32)],
        compiler_params=params(48),
        cost_estimate=cost(4 * 4 * H * 2 * HALF * HALF * HD, 8e6, H * 2 * HALF * HALF),
        name="attend",
    )(meta, q, k, vt)


def back_own_kernel(meta, q, k, kt, v, g, lse, delta, cosine, sine, dq, dk, dv, bias):
    @pl.when(pl.program_id(0) == 0)
    def _():
        own, other = meta[0] * HALF, HALF - meta[0] * HALF
        bias[...] = bias_of(meta, (own, other), 2 * HALF, own)

    parts = []
    for hh in range(2):
        qz = head_part(q[...], hh, HD**-0.5)
        gz = head_part(g[...], hh)
        s = dot_t(k[...], qz) + bias[...]
        p = jnp.exp(s - lse[0, hh : hh + 1, :])
        dp = dot_t(v[...], gz)
        ds = (p * (dp - delta[0, hh : hh + 1, :])).astype(bf16)
        parts.append(dot(kt[hh * HD : (hh + 1) * HD, :], ds) * HD**-0.5)
        gk = dot(ds[:HALF], qz)
        gv = dot(p[:HALF].astype(bf16), gz)
        if hh == 0:
            dk[...] = gk
            dv[...] = gv
        else:
            dk[...] += gk
            dv[...] += gv
    dq[...] = spin(jnp.concatenate(parts, axis=0).T, cosine[...], -sine[...]).astype(bf16)


def back_own_call(meta, q, k, kt, v, g, lse, delta, cosine, sine):
    nat = pl.BlockSpec((HALF, 128), lambda i: (0, i))
    wide = pl.BlockSpec((2 * HALF, 128), lambda i: (0, i))
    row = pl.BlockSpec((1, 2, HALF), lambda i: (i, 0, 0))
    table = pl.BlockSpec((HALF, 128), lambda i: (0, 0))
    return pl.pallas_call(
        back_own_kernel,
        grid=(PAIRS,),
        in_specs=[
            SM,
            nat,
            wide,
            pl.BlockSpec((128, 2 * HALF), lambda i: (i, 0)),
            wide,
            nat,
            row,
            row,
            table,
            table,
        ],
        out_specs=[nat, nat, nat],
        out_shape=[shape((HALF, D), bf16), shape((HALF, D), f32), shape((HALF, D), f32)],
        scratch_shapes=[pltpu.VMEM((2 * HALF, HALF), f32)],
        compiler_params=params(48),
        cost_estimate=cost(4 * 8 * H * 2 * HALF * HALF * HD, 12e6, H * 2 * HALF * HALF),
        name="back_own",
    )(meta, q, k, kt, v, g, lse, delta, cosine, sine)


def back_other_kernel(meta, q, k, v, g, lse, delta, cosine, sine, dk_in, dv_in, dk, dv, bias):
    @pl.when(pl.program_id(0) == 0)
    def _():
        own, other = meta[0] * HALF, HALF - meta[0] * HALF
        bias[...] = bias_of(meta, (own, own), HALF, other)

    gk = dk_in[...]
    gv = dv_in[...]
    for hh in range(2):
        qz = head_part(q[...], hh, HD**-0.5)
        gz = head_part(g[...], hh)
        s = dot_t(k[...], qz) + bias[...]
        p = jnp.exp(s - lse[0, hh : hh + 1, :])
        dp = dot_t(v[...], gz)
        ds = (p * (dp - delta[0, hh : hh + 1, :])).astype(bf16)
        gk = gk + dot(ds, qz)
        gv = gv + dot(p.astype(bf16), gz)
    dk[...] = spin(gk, cosine[...], -sine[...]).astype(bf16)
    dv[...] = gv.astype(bf16)


def back_other_call(meta, q, k, v, g, lse, delta, cosine, sine, dk_in, dv_in):
    nat = pl.BlockSpec((HALF, 128), lambda i: (0, i))
    second = pl.BlockSpec((HALF, 128), lambda i: (1, i))
    row = pl.BlockSpec((1, 2, HALF), lambda i: (i, 0, 0))
    table = pl.BlockSpec((HALF, 128), lambda i: (0, 0))
    return pl.pallas_call(
        back_other_kernel,
        grid=(PAIRS,),
        in_specs=[SM, second, nat, nat, nat, row, row, table, table, nat, nat],
        out_specs=[nat, nat],
        out_shape=[shape((HALF, D), bf16)] * 2,
        scratch_shapes=[pltpu.VMEM((HALF, HALF), f32)],
        compiler_params=params(48),
        cost_estimate=cost(4 * 4 * H * HALF * HALF * HD, 10e6, H * HALF * HALF),
        name="back_other",
    )(meta, q, k, v, g, lse, delta, cosine, sine, dk_in, dv_in)


def norm_parts(r):
    centered = r - jnp.mean(r, axis=-1, keepdims=True)
    scale = lax.rsqrt(jnp.mean(centered * centered, axis=-1, keepdims=True) + norm_eps)
    return centered * scale, scale


def norm_back(c, z, scale, gain):
    e = c * gain
    return (e - jnp.mean(e, axis=-1, keepdims=True) - z * jnp.mean(e * z, axis=-1, keepdims=True)) * scale


def branch_kernel(rows, att, w, res):
    res[...] = rows[...].astype(f32) + dot(att[...], w[0])


def branch_call(rows, att, w1):
    return pl.pallas_call(
        branch_kernel,
        grid=(2,),
        in_specs=[
            pl.BlockSpec((HALF // 2, D), lambda i: (i, 0)),
            pl.BlockSpec((HALF // 2, D), lambda i: (i, 0)),
            pl.BlockSpec((1, D, BLK), lambda i: (1, 0, 1)),
        ],
        out_specs=pl.BlockSpec((HALF // 2, D), lambda i: (i, 0)),
        out_shape=shape((HALF, D), f32),
        compiler_params=params(32),
        cost_estimate=cost(2 * HALF * D * D, 5e6),
        name="branch",
    )(rows, att, w1)


def split_core(c, val):
    parts = val.astype(bf16).reshape(8, 2, 48, val.shape[1])
    return (
        jnp.where(c == 0, parts[:, 0], parts[:, 1]),
        jnp.where(c == 0, parts[:, 1], parts[:, 0]),
    )


def mlp_kernel(meta, res, cot, vecs, wu, wd, *rest):
    pieces = rest[:8]
    (
        out,
        gnorm,
        vgrads,
        keep_g,
        send_g,
        keep_u,
        send_u,
        down_g,
        wg,
        gate,
        up,
        hidden,
        low,
        low_t,
        m,
        acc,
        sems,
    ) = rest[8:]
    step = pl.program_id(0)
    copies = piece_copies(meta, pieces, wg, sems)

    @pl.when(step == 0)
    def _():
        for copy in copies:
            copy.start()
        z, _ = norm_parts(res[...])
        n1 = z * vecs[0:1, :] + vecs[1:2, :]
        acc[...] = n1
        low[...] = n1.astype(bf16)
        low_t[...] = n1.astype(bf16).T
        for copy in copies:
            copy.wait()

    def gate_weight(j):
        return wg[j // 2, :, pl.ds(pl.multiple_of((j % 2) * BLK, BLK), BLK)]

    def up_weight():
        return wu[...].reshape(D, BLK)

    def down_weight():
        slab = wd[...]
        return jnp.concatenate(
            [slab[s, :, r * D : (r + 1) * D] for s in range(4) for r in range(4)], axis=0
        )

    @pl.when(step < 4)
    def _():
        g = dot(low[...], gate_weight(step))
        u = dot(low[...], up_weight())
        h = (g / (1.0 + jnp.exp(-g)) * u).astype(bf16)
        gate[step] = g
        up[step] = u
        hidden[step] = h
        acc[...] += dot(h, down_weight())

    @pl.when(step == 3)
    def _():
        z, scale = norm_parts(acc[...])
        out[...] = (z * vecs[2:3, :] + vecs[3:4, :]).astype(bf16)
        c = cot[...].astype(f32)
        vgrads[0:1, :] = jnp.sum(c * z, axis=0, keepdims=True)
        vgrads[1:2, :] = jnp.sum(c, axis=0, keepdims=True)
        back = norm_back(c, z, scale, vecs[2:3, :])
        acc[...] = back
        m[...] = back.astype(bf16)

    @pl.when(step >= 4)
    def _():
        j = step - 4
        c = meta[3]
        g, u = gate[j], up[j]
        down_g[...] = lax.dot_general(
            hidden[j], m[...], (((0,), (0,)), ((), ())), preferred_element_type=f32
        ).astype(bf16)
        hg = dot_t(m[...], down_weight())
        sig = 1.0 / (1.0 + jnp.exp(-g))
        gate_g = (hg * u * sig * (1.0 + g * (1.0 - sig))).astype(bf16)
        up_g = (hg * g * sig).astype(bf16)
        keep_g[0], send_g[0] = split_core(c, dot(low_t[...], gate_g))
        keep_u[0], send_u[0] = split_core(c, dot(low_t[...], up_g))
        acc[...] += dot_t(gate_g, gate_weight(j)) + dot_t(up_g, up_weight())

    @pl.when(step == 7)
    def _():
        gnorm[...] = acc[...]


def mlp_call(meta, res, cot, vecs, wud, pieces):
    def whole(dims):
        return pl.BlockSpec(dims, lambda i: (0,) * len(dims))

    def late(i):
        return jnp.maximum(i - 4, 0)

    grad = pl.BlockSpec((1, 8, 48, BLK), lambda i: (late(i) // 2, 0, 0, late(i) % 2))
    gshape = shape((2, 8, 48, 2 * BLK), bf16)
    return pl.pallas_call(
        mlp_kernel,
        grid=(8,),
        in_specs=[
            SM,
            whole((HALF, D)),
            whole((HALF, D)),
            whole((8, D)),
            pl.BlockSpec((16, 48, BLK), lambda i: (0, 0, i % 4)),
            pl.BlockSpec((4, 48, FF), lambda i: (i % 4, 1, 0)),
        ]
        + [HBM] * 8,
        out_specs=[
            whole((HALF, D)),
            whole((HALF, D)),
            whole((8, D)),
            grad,
            grad,
            grad,
            grad,
            pl.BlockSpec((BLK, D), lambda i: (late(i), 0)),
        ],
        out_shape=[
            shape((HALF, D), bf16),
            shape((HALF, D), f32),
            shape((8, D), f32),
            gshape,
            gshape,
            gshape,
            gshape,
            shape((FF, D), bf16),
        ],
        scratch_shapes=[
            pltpu.VMEM((2, D, 2 * BLK), bf16),
            pltpu.VMEM((4, HALF, BLK), f32),
            pltpu.VMEM((4, HALF, BLK), f32),
            pltpu.VMEM((4, HALF, BLK), bf16),
            pltpu.VMEM((HALF, D), bf16),
            pltpu.VMEM((D, HALF), bf16),
            pltpu.VMEM((HALF, D), bf16),
            pltpu.VMEM((HALF, D), f32),
            pltpu.SemaphoreType.DMA((32,)),
        ],
        compiler_params=params(60),
        cost_estimate=cost(9 * 2 * HALF * D * FF, 40e6, 2 * HALF * FF),
        name="mlp",
    )(meta, res, cot, vecs, wud, wud, *pieces)


def norm_one_kernel(res, gnorm, vecs, att, w, marks, g_one, low, att_g, delta, vgrads):
    z, scale = norm_parts(res[...])
    c = gnorm[...]
    vgrads[0:1, :] = jnp.sum(c * z, axis=0, keepdims=True)
    vgrads[1:2, :] = jnp.sum(c, axis=0, keepdims=True)
    back = norm_back(c, z, scale, vecs[0:1, :])
    g_one[...] = back
    back = back.astype(bf16)
    low[...] = back
    ag = dot_t(back, w[0]).astype(bf16)
    att_g[...] = ag
    prod = ag.astype(f32) * att[...].astype(f32)
    delta[...] = lax.dot_general(
        marks[...],
        prod,
        (((1,), (1,)), ((), ())),
        preferred_element_type=f32,
        precision=lax.Precision.HIGHEST,
    )


def norm_one_call(res, gnorm, vecs, att, w1, marks):
    def whole(dims):
        return pl.BlockSpec(dims, lambda i: (0,) * len(dims))

    return pl.pallas_call(
        norm_one_kernel,
        grid=(1,),
        in_specs=[
            whole((HALF, D)),
            whole((HALF, D)),
            whole((8, D)),
            whole((HALF, D)),
            pl.BlockSpec((1, D, BLK), lambda i: (1, 0, 1)),
            whole((16, D)),
        ],
        out_specs=[
            whole((HALF, D)),
            whole((HALF, D)),
            whole((HALF, D)),
            whole((16, HALF)),
            whole((8, D)),
        ],
        out_shape=[
            shape((HALF, D), f32),
            shape((HALF, D), bf16),
            shape((HALF, D), bf16),
            shape((16, HALF), f32),
            shape((8, D), f32),
        ],
        compiler_params=params(40),
        cost_estimate=cost(2 * HALF * D * D, 9e6),
        name="norm_one",
    )(res, gnorm, vecs, att, w1, marks)


def first_grads_kernel(meta, rows, att_t, dq, dk, dv, low, keep, send, rows_t):
    step = pl.program_id(0)

    @pl.when(step == 0)
    def _():
        rows_t[...] = rows[...].T

    for j, right in enumerate((dq, dk, dv, low)):

        @pl.when(step == j)
        def _():
            left = att_t[...] if j == 3 else rows_t[...]
            keep[0], send[0] = split_core(meta[3], dot(left, right[...]))


def first_grads_call(meta, rows, att_t, dq, dk, dv, low):
    def whole(dims):
        return pl.BlockSpec(dims, lambda i: (0,) * len(dims))

    grad = pl.BlockSpec((1, 8, 48, BLK), lambda i: (i // 2, 0, 0, i % 2))
    nat = whole((HALF, D))
    return pl.pallas_call(
        first_grads_kernel,
        grid=(4,),
        in_specs=[SM, nat, whole((D, HALF)), nat, nat, nat, nat],
        out_specs=[grad, grad],
        out_shape=[shape((2, 8, 48, 2 * BLK), bf16)] * 2,
        scratch_shapes=[pltpu.VMEM((D, HALF), bf16)],
        compiler_params=params(40),
        cost_estimate=cost(2 * HALF * D * D * 4, 10e6),
        name="first_grads",
    )(meta, rows, att_t, dq, dk, dv, low)


def tokens_grad_kernel(g_one, dq, dk, dv, w, out):
    out[...] = (
        g_one[...]
        + dot_t(dq[...], w[0, :, :D])
        + dot_t(dk[...], w[0, :, D:])
        + dot_t(dv[...], w[1, :, :D])
    )


def tokens_grad_call(g_one, dq, dk, dv, w1):
    part = pl.BlockSpec((HALF // 2, D), lambda i: (i, 0))
    return pl.pallas_call(
        tokens_grad_kernel,
        grid=(2,),
        in_specs=[part, part, part, part, pl.BlockSpec((2, D, 2 * BLK), lambda i: (0, 0, 0))],
        out_specs=part,
        out_shape=shape((HALF, D), f32),
        compiler_params=params(40),
        cost_estimate=cost(2 * HALF * D * D * 3, 12e6),
        name="tokens_grad",
    )(g_one, dq, dk, dv, w1)


def pick(a, at, axis):
    return lax.dynamic_index_in_dim(a, at, axis, keepdims=False)


def flip_x(a):
    return lax.ppermute(a, "seq", [(0, 1), (1, 0)])


def flip(bit):
    def go(a):
        n = lax.axis_size("shard")
        return lax.ppermute(a, "shard", [(s, s ^ bit) for s in range(n)])

    return go


flip_c, flip_y = flip(1), flip(2)


def turn_z(a, k):
    return lax.ppermute(a, "shard", [(s, (s + 4 * k) % 16) for s in range(16)])


def gather_pieces(block, x, y_first):
    mine = pick(block, x, 0)
    a = jnp.stack([mine] + [turn_z(mine, k) for k in (1, 2, 3)])
    if y_first:
        by = flip_y(a)
        bx, bxy = flip_x(a), flip_x(by)
    else:
        bx = flip_x(a)
        by, bxy = flip_y(a), flip_y(bx)
    near = [a, bx, by, bxy]
    return near + [flip_c(t) for t in near]


def pieces_of_whole(full):
    cols = full.shape[1] // 2
    cut = full.reshape(4, 2, 2, 48, 2, cols)
    order = jnp.array([0, 3, 2, 1])
    return [
        cut[:, dy, dc, :, dh][order] for dc in range(2) for dy in range(2) for dh in range(2)
    ]


def add(a, b):
    return a.astype(f32) + b.astype(f32)


def scatter_sum(keep, send, spot, x_first):
    x, z, y = spot
    rows, cols = keep.shape[2:]
    cut = (2, 4, 2, rows, cols)
    got = flip_c(send).reshape(cut)
    kept = keep.reshape(cut)

    def half(at, axis):
        return add(pick(kept, at, axis), pick(got, at, axis))

    if x_first:
        near = add(half(x, 0), flip_x(half(1 - x, 0).astype(bf16)))
        near = add(pick(near, y, 1), flip_y(pick(near, 1 - y, 1).astype(bf16)))
    else:
        near = add(half(y, 2), flip_y(half(1 - y, 2).astype(bf16)))
        near = add(pick(near, x, 0), flip_x(pick(near, 1 - x, 0).astype(bf16)))
    total = pick(near, z, 0)
    for k in (1, 2, 3):
        total = total + turn_z(pick(near, (z + k) % 4, 0).astype(bf16), k).astype(f32)
    total = total.astype(bf16)
    other = flip_x(total)
    return jnp.where(
        x == 0, jnp.stack([total, other]), jnp.stack([other, total])
    ).astype(f32)


def whole_of_split(keep, send):
    both = jnp.stack([keep, send], axis=2)
    return both.transpose(1, 2, 3, 0, 4).reshape(D, -1)


def all_sum_small(v, fast):
    if not fast:
        return lax.psum(v, ("seq", "shard"))
    v = v + flip_x(v)
    v = v + flip_c(v)
    v = v + flip_y(v)
    return v + turn_z(v, 1) + turn_z(v, 2) + turn_z(v, 3)


def gather_small(v, z, y, c):
    a = jnp.stack([v] + [turn_z(v, k) for k in (1, 2, 3)])
    near = jnp.stack([a, flip_y(a)])
    every = jnp.stack([near, flip_c(near)]).astype(f32)
    steps = jnp.arange(4)
    by_z = ((z - steps[:, None]) % 4 == steps[None, :]).astype(f32)
    bits = jnp.arange(2)
    by_y = ((y ^ bits[:, None]) == bits[None, :]).astype(f32)
    by_c = ((c ^ bits[:, None]) == bits[None, :]).astype(f32)
    pick_all = (
        by_z[:, None, None, None, None, :]
        * by_y[None, :, None, None, :, None]
        * by_c[None, None, :, :, None, None]
    )
    out = jnp.sum(pick_all[..., None, None] * every[None, None, None], axis=(3, 4, 5))
    return out.transpose(3, 0, 1, 2, 4).reshape(4, D)


def local(
    tokens,
    doc_lengths,
    qkv_weight,
    out_weight,
    gate_weight,
    up_weight,
    down_weight,
    norm1_gain,
    norm1_bias,
    norm2_gain,
    norm2_bias,
    cotangent,
):
    n = lax.axis_size("shard")
    fast = n == 16
    x = lax.axis_index("seq").astype(jnp.int32)
    shard = lax.axis_index("shard").astype(jnp.int32)
    zero = jnp.zeros((), jnp.int32)
    z, y, c = (shard // 4, (shard // 2) % 2, shard % 2) if fast else (zero, zero, zero)

    rows = tokens[0]
    rows_other = flip_x(rows)

    first_block = jnp.concatenate([qkv_weight, out_weight], axis=1)
    vec_block = jnp.stack([norm1_gain, norm1_bias, norm2_gain, norm2_bias])
    if fast:
        first = jnp.stack([first_block[:, : 2 * BLK], first_block[:, 2 * BLK :]])
        first_pieces = gather_pieces(first, x, True)
        second = jnp.stack([gate_weight[:, : 2 * BLK], gate_weight[:, 2 * BLK :]])
        second, _ = lax.optimization_barrier((second, first_pieces[0]))
        gate_pieces = gather_pieces(second, x, False)
        vecs = gather_small(vec_block, z, y, c)
        slab = jnp.concatenate(
            [
                up_weight,
                down_weight.reshape(4, 48, D).transpose(1, 0, 2).reshape(48, FF),
            ],
            axis=0,
        )
        up_down = lax.all_gather(slab, "shard", axis=0)
    else:
        first_pieces = pieces_of_whole(lax.all_gather(first_block, "shard", axis=0, tiled=True))
        gate_pieces = pieces_of_whole(lax.all_gather(gate_weight, "shard", axis=0, tiled=True))
        vecs = lax.all_gather(vec_block, "shard", axis=1, tiled=True).astype(f32)
        up_all = lax.all_gather(up_weight, "shard", axis=0, tiled=True)
        down_all = lax.all_gather(down_weight, "shard", axis=0, tiled=True)
        up_down = jnp.concatenate(
            [
                up_all.reshape(16, 48, FF),
                down_all.reshape(16, 4, 48, D).transpose(0, 2, 1, 3).reshape(16, 48, FF),
            ],
            axis=1,
        )
    vecs = jnp.pad(vecs.astype(f32), ((0, 4), (0, 0)))

    lengths = lax.dynamic_slice_in_dim(doc_lengths, shard, 1, 0)[0]
    ends = jnp.cumsum(lengths).astype(jnp.int32)
    meta = jnp.concatenate([jnp.stack([x, z, y, c]), jnp.zeros((4,), jnp.int32), ends])
    spots = jnp.arange(2 * HALF, dtype=jnp.int32)
    spots = jnp.where(spots < HALF, spots + x * HALF, spots - x * HALF)
    passed = spots[:, None] >= ends[None, :]
    place = spots - jnp.sum(jnp.where(passed, lengths[None, :], 0), axis=1)
    frequency = rope_base ** (-jnp.arange(HD // 2, dtype=f32) * 2.0 / HD)
    angles = place.astype(f32)[:, None] * frequency[None, :]
    cosine = jnp.tile(jnp.cos(angles), (1, 4))
    sine = jnp.sin(angles)
    sine = jnp.concatenate([-sine, sine, -sine, sine], axis=1)

    q, k, kt, v, vt, w1 = qkv_call(meta, rows, rows_other, cosine, sine, first_pieces)
    att, att_t, lse = attend_call(meta, q, k, vt)
    res = branch_call(rows, att, w1)
    out, gnorm, vg_two, keep_g, send_g, keep_u, send_u, down_g = mlp_call(
        meta, res, cotangent[0], vecs, up_down, gate_pieces
    )
    marks = (
        jnp.arange(16, dtype=jnp.int32)[:, None] == jnp.arange(D, dtype=jnp.int32)[None, :] // HD
    ).astype(f32)
    g_one, g_low, att_g, delta, vg_one = norm_one_call(res, gnorm, vecs, att, w1, marks)
    delta = delta[:H].reshape(PAIRS, 2, HALF)
    stats = jnp.concatenate([lse, delta], axis=0)
    att_g_other = flip_x(att_g)
    stats_other = flip_x(stats)
    vec_grads = all_sum_small(jnp.concatenate([vg_one[:2], vg_two[:2]], axis=0), fast)

    dq, dk, dv = back_own_call(meta, q, k, kt, v, att_g, lse, delta, cosine, sine)
    dk, dv = back_other_call(
        meta, q, k, v, att_g_other, stats_other[:PAIRS], stats_other[PAIRS:], cosine, sine, dk, dv
    )
    keep_f, send_f = first_grads_call(meta, rows, att_t, dq, dk, dv, g_low)
    grad_in = tokens_grad_call(g_one, dq, dk, dv, w1)

    if fast:
        spot = (x, z, y)
        grad_gate = scatter_sum(keep_g, send_g, spot, False)
        grad_up = scatter_sum(keep_u, send_u, spot, True)
        grad_first = scatter_sum(keep_f, send_f, spot, True)
        grad_gate = jnp.concatenate([grad_gate[0], grad_gate[1]], axis=1)
        grad_up = jnp.concatenate([grad_up[0], grad_up[1]], axis=1)
        grad_first = jnp.concatenate([grad_first[0], grad_first[1]], axis=1)
        vec_own = lax.dynamic_slice_in_dim(vec_grads, shard * 48, 48, 1)
    else:
        def owned(a):
            part = lax.psum_scatter(a, "shard", scatter_dimension=0, tiled=True)
            return lax.psum(part, "seq").astype(f32)

        grad_gate = owned(whole_of_split(keep_g, send_g))
        grad_up = owned(whole_of_split(keep_u, send_u))
        grad_first = owned(whole_of_split(keep_f, send_f))
        vec_own = lax.dynamic_slice_in_dim(vec_grads, shard * (D // n), D // n, 1)
    down_part = lax.psum_scatter(down_g, "shard", scatter_dimension=0, tiled=True)
    grad_down = add(down_part, flip_x(down_part))
    return (
        out[None],
        grad_in[None],
        grad_first[:, : 3 * D],
        grad_first[:, 3 * D :],
        grad_gate,
        grad_up,
        grad_down,
        vec_own[0],
        vec_own[1],
        vec_own[2],
        vec_own[3],
    )


def solution(mesh):
    placed = (
        P("shard", "seq", None),
        P(),
        P("shard", None),
        P("shard", None),
        P("shard", None),
        P("shard", None),
        P("shard", None),
        P("shard"),
        P("shard"),
        P("shard"),
        P("shard"),
        P("shard", "seq", None),
    )
    return jax.shard_map(
        local,
        mesh=mesh,
        in_specs=placed,
        out_specs=(
            P("shard", "seq", None),
            P("shard", "seq", None),
            P("shard", None),
            P("shard", None),
            P("shard", None),
            P("shard", None),
            P("shard", None),
            P("shard"),
            P("shard"),
            P("shard"),
            P("shard"),
        ),
        check_vma=False,
    )
```

time: 1020 us -> 425 us (0.42)
  waiting for transfers between devices: 495 us -> 182 us
  matrix products: 154 us -> 0 us
  blocking collectives: 135 us -> 0 us
  Pallas kernels: 0 us -> 107 us
  local copies, waits for them, and re-layouts: 141 us -> 34.1 us
  starting transfers between devices: 13.3 us -> 54.5 us
  loops' own time: 17.9 us -> 0 us
  other arithmetic: 37.7 us -> 24.1 us
    reduce_scatter x4 -> x1, waiting for transfers between devices: 340 us -> 0.02 us  [local(): lax.psum_scatter(down_g, 'shard', scatter_dimension=0, tiled=True)]
    ppermute x0 -> x56, waiting for transfers between devices: none -> 182 us  [the longest x14 76.1 us: flip_x(): return lax.ppermute(a, 'seq', [(0, 1), (1, 0)])]
    dot_general x99 -> x0, matrix products: 154 us -> none  [the longest x24 32.2 us: masked_scores(): jnp.einsum('qd,kd->qk', queries, keys_ctx, preferred_element_type=jnp.flo...]
    pallas_call x0 -> x9, Pallas kernels: none -> 107 us  [the longest x1 38.2 us: mlp_call(): pl.pallas_call(mlp_kernel, grid=(8,), in_specs=[SM, whole((HALF, D)), who...]
    unnamed x2 -> x0, blocking collectives: 92.7 us -> none
    unnamed x12 -> x2, waiting for transfers between devices: 63.6 us -> 0.03 us
    ppermute x0 -> x56, starting transfers between devices: none -> 54.4 us  [the longest x21 30 us: turn_z(): return lax.ppermute(a, 'shard', [(s, (s + 4 * k) % 16) for s in range(16)])]
    all_gather x5 -> x1, waiting for transfers between devices: 48.8 us -> 0.01 us  [local(): up_down = lax.all_gather(slab, 'shard', axis=0)]
  transfers between devices with their start and end apart: 14 -> 58, of which waited for: 7 -> 27; matrix products, arithmetic and copies ran while one was open for 28% -> 7% of each run, Pallas kernels for 0% -> 16%
where the time goes in v1:
time: 425 us; the launch traced here: 417 us
  waiting for transfers between devices  182 us (43%)
  Pallas kernels  107 us (25%)
  starting transfers between devices  54.5 us (13%)
  local copies, waits for them, and re-layouts  34.1 us (8%)
  other arithmetic  24.1 us (6%)
  between operations  15.3 us (4%)
    ppermute x14, waiting for transfers between devices, flip_x(): return lax.ppermute(a, 'seq', [(0, 1), (1, 0)])  76.1 us
    ppermute x21, waiting for transfers between devices, go(): return lax.ppermute(a, 'shard', [(s, s ^ bit) for s in range(n)])  53.2 us
    ppermute x21, waiting for transfers between devices, turn_z(): return lax.ppermute(a, 'shard', [(s, (s + 4 * k) % 16) for s in range(16)])  52.6 us
    pallas_call x1, Pallas kernels, mlp_call(): pl.pallas_call(mlp_kernel, grid=(8,), in_specs=[SM, whole((HALF, D)), who...  38.2 us
    ppermute x21, starting transfers between devices, turn_z(): return lax.ppermute(a, 'shard', [(s, (s + 4 * k) % 16) for s in range(16)])  30 us
    unnamed x102, local copies, waits for them, and re-layouts  24.2 us
    pallas_call x1, Pallas kernels, back_own_call(): pl.pallas_call(back_own_kernel, grid=(PAIRS,), in_specs=[SM, nat, wide, p...  17.5 us
    pallas_call x1, Pallas kernels, attend_call(): pl.pallas_call(attend_kernel, grid=(PAIRS,), in_specs=[SM, pl.BlockSpec((...  14.4 us
  transfers between devices with their start and end apart: 58, of which 27 were waited for; matrix products, arithmetic and copies ran while one was open for 7% of the time, Pallas kernels for 16%

profile of v1, /device:TPU:0, one launch (start us, length us, event | category | flops | bytes accessed | tf_op | source)
XLA Modules:
  0.0 416.8 jit_solution(11901914714669574501)
XLA Ops:
  8.3 1.9 pad_maximum_fusion.1
  10.4 3.1 collective-permute-start.1
  13.5 2.6 collective-permute-start.2
  16.2 1.8 collective-permute-start.12
  18.0 1.9 collective-permute-start.13
  21.8 3.0 fusion.18
  29.0 2.1 collective-permute-done.14
  31.1 6.8 %collective-permute-done.3 = bf16[48,1536]{1,0:T(8,128)(2,1)S(1)} collective-permute-done((bf16[48,1536]{1,0:T(8,128)(2,1)S(1)}, bf16[48,1536]{1,0:T(8,128)(2,1)S(1)}, u32[]{:S(2)}, u32[]{:S(2)}) %collective-permute-start.3) | collective-permute-done | bytes 147488 | tf_op jit(solution)/shard_map/ppermute | solution.py:631
  40.0 3.1 collective-permute-start.18
  43.1 7.8 %collective-permute-done.16 = bf16[48,1536]{1,0:T(8,128)(2,1)S(1)} collective-permute-done((bf16[48,1536]{1,0:T(8,128)(2,1)S(1)}, bf16[48,1536]{1,0:T(8,128)(2,1)S(1)}, u32[]{:S(2)}, u32[]{:S(2)}) %collective-permute-start.16) | collective-permute-done | bytes 147488 | tf_op jit(solution)/shard_map/ppermute | solution.py:631
  50.9 6.9 %collective-permute-done.17 = bf16[48,1536]{1,0:T(8,128)(2,1)S(1)} collective-permute-done((bf16[48,1536]{1,0:T(8,128)(2,1)S(1)}, bf16[48,1536]{1,0:T(8,128)(2,1)S(1)}, u32[]{:S(2)}, u32[]{:S(2)}) %collective-permute-start.17) | collective-permute-done | bytes 147488 | tf_op jit(solution)/shard_map/ppermute | solution.py:631
  63.3 2.1 pad_maximum_fusion.5.sine
  66.9 7.3 %collective-permute-done.4.rest_1_ = bf16[4,48,1536]{2,1,0:T(8,128)(2,1)} collective-permute-done((bf16[4,48,1536]{2,1,0:T(8,128)(2,1)S(1)}, bf16[4,48,1536]{2,1,0:T(8,128)(2,1)}, u32[]{:S(2)}, u32[]{:S(2)}) %collective-permute-start.4) | collective-permute-done | bytes 589856 | tf_op jit(solution)/shard_map/ppermute | solution.py:616
  74.3 1.6 collective-permute-start.20
  77.2 9.7 %collective-permute-done.19.rest_1_ = bf16[4,48,1536]{2,1,0:T(8,128)(2,1)} collective-permute-done((bf16[4,48,1536]{2,1,0:T(8,128)(2,1)}, bf16[4,48,1536]{2,1,0:T(8,128)(2,1)}, u32[]{:S(2)}, u32[]{:S(2)}) %collective-permute-start.19) | collective-permute-done | bytes 589856 | tf_op jit(solution)/shard_map/ppermute | solution.py:616
  88.5 9.0 %collective-permute-done.6.rest_3_ = bf16[4,48,1536]{2,1,0:T(8,128)(2,1)} collective-permute-done((bf16[4,48,1536]{2,1,0:T(8,128)(2,1)}, bf16[4,48,1536]{2,1,0:T(8,128)(2,1)}, u32[]{:S(2)}, u32[]{:S(2)}) %collective-permute-start.6) | collective-permute-done | bytes 589856 | tf_op jit(solution)/shard_map/ppermute | solution.py:616
  100.2 3.2 collective-permute-done.20.rest_2_
  104.0 13.0 %collective-permute-done.21.rest_3_ = bf16[4,48,1536]{2,1,0:T(8,128)(2,1)} collective-permute-done((bf16[4,48,1536]{2,1,0:T(8,128)(2,1)}, bf16[4,48,1536]{2,1,0:T(8,128)(2,1)}, u32[]{:S(2)}, u32[]{:S(2)}) %collective-permute-start.21) | collective-permute-done | bytes 589856 | tf_op jit(solution)/shard_map/ppermute | solution.py:622
  118.1 14.0 %qkv.1 = (bf16[1024,768]{1,0:T(8,128)(2,1)}, bf16[1024,768]{1,0:T(8,128)(2,1)}, bf16[768,1024]{1,0:T(8,128)(2,1)}, bf16[1024,768]{1,0:T(8,128)(2,1)}, bf16[768,1...) custom-call(s32[16]{0:T(128)S(1)} %concatenate.31.meta, bf16[512,768]{1,0:T(8,128)(2,1)} %bitcast.160, ...), custom_call_target="tpu_custom_call" | custom-call | flops 3623878656 | bytes 20000000 | tf_op jit(solution)/shard_map/qkv/pallas_call | solution.py:119
  135.2 14.4 %attend.1 = (bf16[512,768]{1,0:T(8,128)(2,1)S(1)}, bf16[768,512]{1,0:T(8,128)(2,1)S(1)}, f32[6,2,512]{2,1,0:T(2,128)S(1)}) custom-call(s32[16]{0:T(128)S(1)} %concatenate.31.meta, bf16[1024,768]{1,0:T(8,128)(2,1)S(1)} %copy-done.28, bf16[1024,768]{1,0:T(8,128)(2,1)S(1)} %copy-done.30, bf16[768,1024]{1,0:T(8,128)(2,1)} %get-tuple-element.43.vt), custom_call_target="tpu_custom_call" | custom-call | flops 6442450944 | bytes 8000000 | tf_op jit(solution)/shard_map/attend/pallas_call | solution.py:190
  154.4 38.2 %mlp.1 = (bf16[512,768]{1,0:T(8,128)(2,1)}, f32[512,768]{1,0:T(8,128)}, f32[8,768]{1,0:T(8,128)}, bf16[2,8,48,1536]{3,2,1,0:T(8,128)(2,1)}, bf16[2,8,48,1536]{3,...) custom-call(s32[16]{0:T(128)} %copy-done.20, ...), custom_call_target="tpu_custom_call" | custom-call | flops 21743271936 | bytes 40000000 | tf_op jit(solution)/shard_map/mlp/pallas_call | solution.py:449
  193.3 2.3 copy-done.2
  197.0 3.0 norm_one.1
  209.5 17.5 %back_own.1 = (bf16[512,768]{1,0:T(8,128)(2,1)S(1)}, f32[512,768]{1,0:T(8,128)S(1)}, f32[512,768]{1,0:T(8,128)S(1)}) custom-call(s32[16]{0:T(128)S(1)} %copy-done.21, bf16[1024,768]{1,0:T(8,128)(2,1)} %get-tuple-element.41.q, bf16[1024,768]{1,0:T(8,128)(2,1)} %get-tuple-element.42.k, bf16[768,1024]{1,0:T(8,128)(2,1)} %get-tuple-element.50.kt, ...), custom_call_target="tpu_custom_call" | custom-call | flops 12884901888 | bytes 12000000 | tf_op jit(solution)/shard_map/back_own/pallas_call | solution.py:247
  229.4 10.6 %back_other.1 = (bf16[512,768]{1,0:T(8,128)(2,1)S(1)}, bf16[512,768]{1,0:T(8,128)(2,1)S(1)}) custom-call(s32[16]{0:T(128)S(1)} %copy-done.21, bf16[1024,768]{1,0:T(8,128)(2,1)S(1)} %copy-done.29, bf16[1024,768]{1,0:T(8,128)(2,1)} %get-tuple-element.42.k, bf16[1024,768]{1,0:T(8,128)(2,1)} %get-tuple-element.51.v, ...), custom_call_target="tpu_custom_call" | custom-call | flops 3221225472 | bytes 10000000 | tf_op jit(solution)/shard_map/back_other/pallas_call | solution.py:297
  240.1 5.0 %first_grads.1 = (bf16[2,8,48,1536]{3,2,1,0:T(8,128)(2,1)S(1)}, bf16[2,8,48,1536]{3,2,1,0:T(8,128)(2,1)}) custom-call(s32[16]{0:T(128)S(1)} %copy-done.21, bf16[512,768]{1,0:T(8,128)(2,1)S(1)} %bitcast.163, bf16[768,512]{1,0:T(8,128)(2,1)S(1)} %copy-done.34, bf16[512,768]{1,0:T(8,128)(2,1)S(1)} %get-tuple-element.55.dq, ...), custom_call_target="tpu_custom_call" | custom-call | flops 2415919104 | bytes 10000000 | tf_op jit(solution)/shard_map/first_grads/pallas_call | solution.py:575
  245.5 2.7 fusion.1
  251.6 25.1 %collective-permute-done.52 = f32[4,768]{1,0:T(4,128)S(1)} collective-permute-done((f32[4,768]{1,0:T(4,128)S(1)}, f32[4,768]{1,0:T(4,128)S(1)}, u32[]{:S(2)}, u32[]{:S(2)}) %collective-permute-start.52) | collective-permute-done | bytes 12320 | tf_op jit(solution)/shard_map/ppermute | solution.py:622
  278.3 2.3 collective-permute-start.54
  283.7 2.1 constant_dynamic-slice_fusion.4
  286.6 2.6 copy-done.3
  289.2 3.1 tokens_grad.1
  292.5 1.6 copy-done.36
  294.1 2.2 bitcast_add_fusion.1
  297.1 2.7 constant_dynamic-slice_fusion.3
  301.6 11.1 %collective-permute-done.37 = bf16[4,48,1536]{2,1,0:T(8,128)(2,1)S(1)} collective-permute-done((bf16[4,48,1536]{2,1,0:T(8,128)(2,1)S(1)}, bf16[4,48,1536]{2,1,0:T(8,128)(2,1)S(1)}, u32[]{:S(2)}, u32[]{:S(2)}) %collective-permute-start.37) | collective-permute-done | bytes 589856 | tf_op jit(solution)/shard_map/ppermute | solution.py:616
  313.5 3.3 collective-permute-start.39
  318.1 6.6 %collective-permute-done.38 = bf16[48,1536]{1,0:T(8,128)(2,1)S(1)} collective-permute-done((bf16[48,1536]{1,0:T(8,128)(2,1)S(1)}, bf16[48,1536]{1,0:T(8,128)(2,1)S(1)}, u32[]{:S(2)}, u32[]{:S(2)}) %collective-permute-start.38) | collective-permute-done | bytes 147488 | tf_op jit(solution)/shard_map/ppermute | solution.py:631
  324.6 7.5 %collective-permute-done.39 = bf16[48,1536]{1,0:T(8,128)(2,1)S(1)} collective-permute-done((bf16[48,1536]{1,0:T(8,128)(2,1)S(1)}, bf16[48,1536]{1,0:T(8,128)(2,1)S(1)}, u32[]{:S(2)}, u32[]{:S(2)}) %collective-permute-start.39) | collective-permute-done | bytes 147488 | tf_op jit(solution)/shard_map/ppermute | solution.py:631
  332.8 5.2 %collective-permute-done.43 = bf16[4,2,48,1536]{3,2,0,1:T(8,128)(2,1)S(1)} collective-permute-done((bf16[4,2,48,1536]{3,2,0,1:T(8,128)(2,1)S(1)}, bf16[4,2,48,1536]{3,2,0,1:T(8,128)(2,1)S(1)}, u32[]{:S(2)}, u32[]{:S(2)}) %collective-permute-start.43) | collective-permute-done | bytes 1179680 | tf_op jit(solution)/shard_map/ppermute | solution.py:616
  339.2 22.4 %collective-permute-done.29 = bf16[4,2,48,1536]{3,2,0,1:T(8,128)(2,1)S(1)} collective-permute-done((bf16[4,2,48,1536]{3,2,0,1:T(8,128)(2,1)S(1)}, bf16[4,2,48,1536]{3,2,0,1:T(8,128)(2,1)S(1)}, u32[]{:S(2)}, u32[]{:S(2)}) %collective-permute-start.29) | collective-permute-done | bytes 1179680 | tf_op jit(solution)/shard_map/ppermute | solution.py:616
  364.0 8.6 %collective-permute-done.30 = bf16[4,48,1536]{2,1,0:T(8,128)(2,1)S(1)} collective-permute-done((bf16[4,48,1536]{2,1,0:T(8,128)(2,1)S(1)}, bf16[4,48,1536]{2,1,0:T(8,128)(2,1)S(1)}, u32[]{:S(2)}, u32[]{:S(2)}) %collective-permute-start.30) | collective-permute-done | bytes 589856 | tf_op jit(solution)/shard_map/ppermute | solution.py:622
  373.6 1.8 collective-permute-start.32
  379.1 2.4 collective-permute-done.31
  381.9 7.3 %collective-permute-done.32 = bf16[48,1536]{1,0:T(8,128)(2,1)S(1)} collective-permute-done((bf16[48,1536]{1,0:T(8,128)(2,1)S(1)}, bf16[48,1536]{1,0:T(8,128)(2,1)S(1)}, u32[]{:S(2)}, u32[]{:S(2)}) %collective-permute-start.32) | collective-permute-done | bytes 147488 | tf_op jit(solution)/shard_map/ppermute | solution.py:631
  389.8 5.2 %collective-permute-done.46 = bf16[48,1536]{1,0:T(8,128)(2,1)S(1)} collective-permute-done((bf16[48,1536]{1,0:T(8,128)(2,1)S(1)}, bf16[48,1536]{1,0:T(8,128)(2,1)S(1)}, u32[]{:S(2)}, u32[]{:S(2)}) %collective-permute-start.46) | collective-permute-done | bytes 147488 | tf_op jit(solution)/shard_map/ppermute | solution.py:631
  396.0 4.7 %collective-permute-done.48 = bf16[48,1536]{1,0:T(8,128)(2,1)S(1)} collective-permute-done((bf16[48,1536]{1,0:T(8,128)(2,1)S(1)}, bf16[48,1536]{1,0:T(8,128)(2,1)S(1)}, u32[]{:S(2)}, u32[]{:S(2)}) %collective-permute-start.48) | collective-permute-done | bytes 147488 | tf_op jit(solution)/shard_map/ppermute | solution.py:616
  402.6 6.1 %collective-permute-done.49 = bf16[192,768]{1,0:T(8,128)(2,1)S(1)} collective-permute-done((bf16[192,768]{1,0:T(8,128)(2,1)}, bf16[192,768]{1,0:T(8,128)(2,1)S(1)}, u32[]{:S(2)}, u32[]{:S(2)}) %collective-permute-start.49) | collective-permute-done | bytes 294944 | tf_op jit(solution)/shard_map/ppermute | solution.py:616
  (268 shorter events, 73.1 us)
Async XLA Ops:
  7.2 147.2 %all-gather.3.cloned.1.call-start = ((), (), s32[]{:S(2)}) async-start(), calls=%async_computation.2 | async-start | bytes 10027008 | tf_op jit(solution)/shard_map/all_gather | solution.py:758
  10.2 391.5 %reduce-scatter.2.cloned.1.call-start = ((), (), s32[]{:S(2)}) async-start(), calls=%async_computation.1 | async-start | bytes 5013504 | tf_op jit(solution)/shard_map/reduce_scatter | solution.py:828
  10.4 20.7 %collective-permute-start.1 = (bf16[48,1536]{1,0:T(8,128)(2,1)S(1)}, bf16[48,1536]{1,0:T(8,128)(2,1)S(1)}, u32[]{:S(2)}, u32[]{:S(2)}) collective-permute-start(bf16[48,1536]{1,0:T(8,128)(2,1)S(1)} %bitcast.171), channel_id=1, source_target_pairs={{0,4},{1,5},{2,6},{3,7},{4,8},{5,9},{6,10},{7,11},{8,12},{9,13},{1... | collective-permute-start | bytes 442376 | tf_op jit(solution)/shard_map/ppermute | solution.py:631
  13.5 17.6 %collective-permute-start.2 = (bf16[48,1536]{1,0:T(8,128)(2,1)S(1)}, bf16[48,1536]{1,0:T(8,128)(2,1)S(1)}, u32[]{:S(2)}, u32[]{:S(2)}) collective-permute-start(bf16[48,1536]{1,0:T(8,128)(2,1)S(1)} %bitcast.172), channel_id=1, source_target_pairs={{0,8},{1,9},{2,10},{3,11},{4,12},{5,13},{6,14},{7,15},{8,0},{9,1},... | collective-permute-start | bytes 442376 | tf_op jit(solution)/shard_map/ppermute | solution.py:631
  16.2 9.6 %collective-permute-start.12 = (bf16[4,48]{1,0:T(4,128)(2,1)S(1)}, bf16[4,48]{1,0:T(4,128)(2,1)S(1)}, u32[]{:S(2)}, u32[]{:S(2)}) collective-permute-start(bf16[4,48]{1,0:T(4,128)(2,1)S(1)} %pad_maximum_fusion.13), channel_id=1, source_target_pairs={{0,8},{1,9},{2,10},{3,11},{4,12},{5,13},{6,14},{7,15},{8,0},{9,1},... | collective-permute-start | bytes 1160 | tf_op jit(solution)/shard_map/ppermute | solution.py:631
  18.0 9.3 %collective-permute-start.13 = (bf16[4,48]{1,0:T(4,128)(2,1)S(1)}, bf16[4,48]{1,0:T(4,128)(2,1)S(1)}, u32[]{:S(2)}, u32[]{:S(2)}) collective-permute-start(bf16[4,48]{1,0:T(4,128)(2,1)S(1)} %pad_maximum_fusion.13), channel_id=1, source_target_pairs={{0,12},{1,13},{2,14},{3,15},{4,0},{5,1},{6,2},{7,3},{8,4},{9,5},{1... | collective-permute-start | bytes 1160 | tf_op jit(solution)/shard_map/ppermute | solution.py:631
  24.8 13.1 %collective-permute-start.3 = (bf16[48,1536]{1,0:T(8,128)(2,1)S(1)}, bf16[48,1536]{1,0:T(8,128)(2,1)S(1)}, u32[]{:S(2)}, u32[]{:S(2)}) collective-permute-start(bf16[48,1536]{1,0:T(8,128)(2,1)S(1)} %bitcast.173), channel_id=1, source_target_pairs={{0,12},{1,13},{2,14},{3,15},{4,0},{5,1},{6,2},{7,3},{8,4},{9,5},{1... | collective-permute-start | bytes 442376 | tf_op jit(solution)/shard_map/ppermute | solution.py:631
  25.9 50.8 %collective-permute-start = (bf16[512,768]{1,0:T(8,128)(2,1)S(1)}, bf16[512,768]{1,0:T(8,128)(2,1)}, u32[]{:S(2)}, u32[]{:S(2)}) collective-permute-start(bf16[512,768]{1,0:T(8,128)(2,1)S(1)} %bitcast.161), channel_id=1, source_target_pairs={{0,16},{16,0},{1,17},{17,1},{2,18},{18,2},{3,19},{19,3},{4,20},{20... | collective-permute-start | bytes 2359304 | tf_op jit(solution)/shard_map/ppermute | solution.py:616
  38.0 22.8 %collective-permute-start.5 = (bf16[4,48,1536]{2,1,0:T(8,128)(2,1)S(1)}, bf16[4,48,1536]{2,1,0:T(8,128)(2,1)}, u32[]{:S(2)}, u32[]{:S(2)}) collective-permute-start(bf16[4,48,1536]{2,1,0:T(8,128)(2,1)S(1)} %pad_maximum_fusion.rest_0_), channel_id=1, source_target_pairs={{0,2},{1,3},{2,0},{3,1},{4,6},{5,7},{6,4},{7,5},{8,10},{9,11},{10,... | collective-permute-start | bytes 1769480 | tf_op jit(solution)/shard_map/ppermute | solution.py:622
  39.2 11.7 %collective-permute-start.16 = (bf16[48,1536]{1,0:T(8,128)(2,1)S(1)}, bf16[48,1536]{1,0:T(8,128)(2,1)S(1)}, u32[]{:S(2)}, u32[]{:S(2)}) collective-permute-start(bf16[48,1536]{1,0:T(8,128)(2,1)S(1)} %fusion.43), channel_id=1, source_target_pairs={{0,4},{1,5},{2,6},{3,7},{4,8},{5,9},{6,10},{7,11},{8,12},{9,13},{1... | collective-permute-start | bytes 442376 | tf_op jit(solution)/shard_map/ppermute | solution.py:631
  40.0 17.8 %collective-permute-start.17 = (bf16[48,1536]{1,0:T(8,128)(2,1)S(1)}, bf16[48,1536]{1,0:T(8,128)(2,1)S(1)}, u32[]{:S(2)}, u32[]{:S(2)}) collective-permute-start(bf16[48,1536]{1,0:T(8,128)(2,1)S(1)} %fusion.43), channel_id=1, source_target_pairs={{0,8},{1,9},{2,10},{3,11},{4,12},{5,13},{6,14},{7,15},{8,0},{9,1},... | collective-permute-start | bytes 442376 | tf_op jit(solution)/shard_map/ppermute | solution.py:631
  40.0 19.4 %collective-permute-start.18 = (bf16[48,1536]{1,0:T(8,128)(2,1)S(1)}, bf16[48,1536]{1,0:T(8,128)(2,1)S(1)}, u32[]{:S(2)}, u32[]{:S(2)}) collective-permute-start(bf16[48,1536]{1,0:T(8,128)(2,1)S(1)} %fusion.43), channel_id=1, source_target_pairs={{0,12},{1,13},{2,14},{3,15},{4,0},{5,1},{6,2},{7,3},{8,4},{9,5},{1... | collective-permute-start | bytes 442376 | tf_op jit(solution)/shard_map/ppermute | solution.py:631
  50.9 9.4 %collective-permute-start.15 = (bf16[2,4,4,48]{3,2,1,0:T(4,128)(2,1)S(1)}, bf16[2,4,4,48]{3,2,1,0:T(4,128)(2,1)S(1)}, u32[]{:S(2)}, u32[]{:S(2)}) collective-permute-start(bf16[2,4,4,48]{3,2,1,0:T(4,128)(2,1)S(1)} %get-tuple-element.101), channel_id=1, source_target_pairs={{0,1},{1,0},{2,3},{3,2},{4,5},{5,4},{6,7},{7,6},{8,9},{9,8},{10,11... | collective-permute-start | bytes 9224 | tf_op jit(solution)/shard_map/ppermute | solution.py:622
  57.9 16.4 %collective-permute-start.4 = (bf16[4,48,1536]{2,1,0:T(8,128)(2,1)S(1)}, bf16[4,48,1536]{2,1,0:T(8,128)(2,1)}, u32[]{:S(2)}, u32[]{:S(2)}) collective-permute-start(bf16[4,48,1536]{2,1,0:T(8,128)(2,1)S(1)} %pad_maximum_fusion.rest_0_), channel_id=1, source_target_pairs={{0,16},{16,0},{1,17},{17,1},{2,18},{18,2},{3,19},{19,3},{4,20},{20... | collective-permute-start | bytes 1769480 | tf_op jit(solution)/shard_map/ppermute | solution.py:616
  59.4 16.4 %collective-permute-start.7 = (bf16[4,48,1536]{2,1,0:T(8,128)(2,1)S(1)}, bf16[4,48,1536]{2,1,0:T(8,128)(2,1)S(1)}, u32[]{:S(2)}, u32[]{:S(2)}) collective-permute-start(bf16[4,48,1536]{2,1,0:T(8,128)(2,1)S(1)} %pad_maximum_fusion.rest_0_), channel_id=1, source_target_pairs={{0,1},{1,0},{2,3},{3,2},{4,5},{5,4},{6,7},{7,6},{8,9},{9,8},{10,11... | collective-permute-start | bytes 1769480 | tf_op jit(solution)/shard_map/ppermute | solution.py:622
  60.3 26.6 %collective-permute-start.19 = (bf16[4,48,1536]{2,1,0:T(8,128)(2,1)}, bf16[4,48,1536]{2,1,0:T(8,128)(2,1)}, u32[]{:S(2)}, u32[]{:S(2)}) collective-permute-start(bf16[4,48,1536]{2,1,0:T(8,128)(2,1)} %pad_maximum_fusion.2.rest_0_), channel_id=1, source_target_pairs={{0,16},{16,0},{1,17},{17,1},{2,18},{18,2},{3,19},{19,3},{4,20},{20... | collective-permute-start | bytes 1769480 | tf_op jit(solution)/shard_map/ppermute | solution.py:616
  60.8 36.7 %collective-permute-start.6 = (bf16[4,48,1536]{2,1,0:T(8,128)(2,1)}, bf16[4,48,1536]{2,1,0:T(8,128)(2,1)}, u32[]{:S(2)}, u32[]{:S(2)}) collective-permute-start(bf16[4,48,1536]{2,1,0:T(8,128)(2,1)} %collective-permute-done.5.rest_2_), channel_id=1, source_target_pairs={{0,16},{16,0},{1,17},{17,1},{2,18},{18,2},{3,19},{19,3},{4,20},{20... | collective-permute-start | bytes 1769480 | tf_op jit(solution)/shard_map/ppermute | solution.py:616
  74.3 29.1 %collective-permute-start.20 = (bf16[4,48,1536]{2,1,0:T(8,128)(2,1)}, bf16[4,48,1536]{2,1,0:T(8,128)(2,1)}, u32[]{:S(2)}, u32[]{:S(2)}) collective-permute-start(bf16[4,48,1536]{2,1,0:T(8,128)(2,1)} %pad_maximum_fusion.2.rest_0_), channel_id=1, source_target_pairs={{0,2},{1,3},{2,0},{3,1},{4,6},{5,7},{6,4},{7,5},{8,10},{9,11},{10,... | collective-permute-start | bytes 1769480 | tf_op jit(solution)/shard_map/ppermute | solution.py:622
  76.7 26.7 %collective-permute-start.9 = (bf16[4,48,1536]{2,1,0:T(8,128)(2,1)}, bf16[4,48,1536]{2,1,0:T(8,128)(2,1)}, u32[]{:S(2)}, u32[]{:S(2)}) collective-permute-start(bf16[4,48,1536]{2,1,0:T(8,128)(2,1)} %collective-permute-done.5.rest_2_), channel_id=1, source_target_pairs={{0,1},{1,0},{2,3},{3,2},{4,5},{5,4},{6,7},{7,6},{8,9},{9,8},{10,11... | collective-permute-start | bytes 1769480 | tf_op jit(solution)/shard_map/ppermute | solution.py:622
  76.7 27.2 %collective-permute-start.8 = (bf16[4,48,1536]{2,1,0:T(8,128)(2,1)}, bf16[4,48,1536]{2,1,0:T(8,128)(2,1)S(1)}, u32[]{:S(2)}, u32[]{:S(2)}) collective-permute-start(bf16[4,48,1536]{2,1,0:T(8,128)(2,1)} %collective-permute-done.4.rest_1_), channel_id=1, source_target_pairs={{0,1},{1,0},{2,3},{3,2},{4,5},{5,4},{6,7},{7,6},{8,9},{9,8},{10,11... | collective-permute-start | bytes 1769480 | tf_op jit(solution)/shard_map/ppermute | solution.py:622
  86.9 30.1 %collective-permute-start.21 = (bf16[4,48,1536]{2,1,0:T(8,128)(2,1)}, bf16[4,48,1536]{2,1,0:T(8,128)(2,1)}, u32[]{:S(2)}, u32[]{:S(2)}) collective-permute-start(bf16[4,48,1536]{2,1,0:T(8,128)(2,1)} %collective-permute-done.19.rest_1_), channel_id=1, source_target_pairs={{0,2},{1,3},{2,0},{3,1},{4,6},{5,7},{6,4},{7,5},{8,10},{9,11},{10,... | collective-permute-start | bytes 1769480 | tf_op jit(solution)/shard_map/ppermute | solution.py:622
  97.5 19.5 %collective-permute-start.10 = (bf16[4,48,1536]{2,1,0:T(8,128)(2,1)}, bf16[4,48,1536]{2,1,0:T(8,128)(2,1)}, u32[]{:S(2)}, u32[]{:S(2)}) collective-permute-start(bf16[4,48,1536]{2,1,0:T(8,128)(2,1)} %collective-permute-done.6.rest_3_), channel_id=1, source_target_pairs={{0,1},{1,0},{2,3},{3,2},{4,5},{5,4},{6,7},{7,6},{8,9},{9,8},{10,11... | collective-permute-start | bytes 1769480 | tf_op jit(solution)/shard_map/ppermute | solution.py:622
  103.4 48.6 %collective-permute-start.22 = (bf16[4,48,1536]{2,1,0:T(8,128)(2,1)}, bf16[4,48,1536]{2,1,0:T(8,128)(2,1)S(1)}, u32[]{:S(2)}, u32[]{:S(2)}) collective-permute-start(bf16[4,48,1536]{2,1,0:T(8,128)(2,1)} %pad_maximum_fusion.2.rest_0_), channel_id=1, source_target_pairs={{0,1},{1,0},{2,3},{3,2},{4,5},{5,4},{6,7},{7,6},{8,9},{9,8},{10,11... | collective-permute-start | bytes 1769480 | tf_op jit(solution)/shard_map/ppermute | solution.py:622
  103.4 49.4 %collective-permute-start.23 = (bf16[4,48,1536]{2,1,0:T(8,128)(2,1)}, bf16[4,48,1536]{2,1,0:T(8,128)(2,1)S(1)}, u32[]{:S(2)}, u32[]{:S(2)}) collective-permute-start(bf16[4,48,1536]{2,1,0:T(8,128)(2,1)} %collective-permute-done.19.rest_1_), channel_id=1, source_target_pairs={{0,1},{1,0},{2,3},{3,2},{4,5},{5,4},{6,7},{7,6},{8,9},{9,8},{10,11... | collective-permute-start | bytes 1769480 | tf_op jit(solution)/shard_map/ppermute | solution.py:622
  103.9 49.7 %collective-permute-start.24 = (bf16[4,48,1536]{2,1,0:T(8,128)(2,1)}, bf16[4,48,1536]{2,1,0:T(8,128)(2,1)S(1)}, u32[]{:S(2)}, u32[]{:S(2)}) collective-permute-start(bf16[4,48,1536]{2,1,0:T(8,128)(2,1)} %collective-permute-done.20.rest_2_), channel_id=1, source_target_pairs={{0,1},{1,0},{2,3},{3,2},{4,5},{5,4},{6,7},{7,6},{8,9},{9,8},{10,11... | collective-permute-start | bytes 1769480 | tf_op jit(solution)/shard_map/ppermute | solution.py:622
  117.0 37.4 %collective-permute-start.25 = (bf16[4,48,1536]{2,1,0:T(8,128)(2,1)}, bf16[4,48,1536]{2,1,0:T(8,128)(2,1)}, u32[]{:S(2)}, u32[]{:S(2)}) collective-permute-start(bf16[4,48,1536]{2,1,0:T(8,128)(2,1)} %collective-permute-done.21.rest_3_), channel_id=1, source_target_pairs={{0,1},{1,0},{2,3},{3,2},{4,5},{5,4},{6,7},{7,6},{8,9},{9,8},{10,11... | collective-permute-start | bytes 1769480 | tf_op jit(solution)/shard_map/ppermute | solution.py:622
  192.6 52.9 %collective-permute-start.35 = (bf16[2,8,48,1536]{3,2,1,0:T(8,128)(2,1)}, bf16[2,8,48,1536]{3,2,1,0:T(8,128)(2,1)}, u32[]{:S(2)}, u32[]{:S(2)}) collective-permute-start(bf16[2,8,48,1536]{3,2,1,0:T(8,128)(2,1)} %get-tuple-element.65), channel_id=1, source_target_pairs={{0,1},{1,0},{2,3},{3,2},{4,5},{5,4},{6,7},{7,6},{8,9},{9,8},{10,11... | collective-permute-start | bytes 7077896 | tf_op jit(solution)/shard_map/ppermute | solution.py:622
  203.7 45.2 %collective-permute-start.50 = (f32[4,768]{1,0:T(4,128)S(1)}, f32[4,768]{1,0:T(4,128)S(1)}, u32[]{:S(2)}, u32[]{:S(2)}) collective-permute-start(f32[4,768]{1,0:T(4,128)S(1)} %pad_maximum_fusion.10), channel_id=1, source_target_pairs={{0,16},{16,0},{1,17},{17,1},{2,18},{18,2},{3,19},{19,3},{4,20},{20... | collective-permute-start | bytes 36872 | tf_op jit(solution)/shard_map/ppermute | solution.py:616
  205.2 24.1 %collective-permute-start.27 = (f32[12,2,512]{2,1,0:T(2,128)S(1)}, f32[12,2,512]{2,1,0:T(2,128)S(1)}, u32[]{:S(2)}, u32[]{:S(2)}) collective-permute-start(f32[12,2,512]{2,1,0:T(2,128)S(1)} %pad_maximum_fusion.9), channel_id=1, source_target_pairs={{0,16},{16,0},{1,17},{17,1},{2,18},{18,2},{3,19},{19,3},{4,20},{20... | collective-permute-start | bytes 147464 | tf_op jit(solution)/shard_map/ppermute | solution.py:616
  205.9 23.4 %collective-permute-start.26 = (bf16[512,768]{1,0:T(8,128)(2,1)}, bf16[512,768]{1,0:T(8,128)(2,1)S(1)}, u32[]{:S(2)}, u32[]{:S(2)}) collective-permute-start(bf16[512,768]{1,0:T(8,128)(2,1)} %copy-done.24), channel_id=1, source_target_pairs={{0,16},{16,0},{1,17},{17,1},{2,18},{18,2},{3,19},{19,3},{4,20},{20... | collective-permute-start | bytes 2359304 | tf_op jit(solution)/shard_map/ppermute | solution.py:616
  207.3 89.8 %collective-permute-start.42 = (bf16[2,8,48,1536]{3,2,1,0:T(8,128)(2,1)}, bf16[2,8,48,1536]{3,2,1,0:T(8,128)(2,1)}, u32[]{:S(2)}, u32[]{:S(2)}) collective-permute-start(bf16[2,8,48,1536]{3,2,1,0:T(8,128)(2,1)} %get-tuple-element.67), channel_id=1, source_target_pairs={{0,1},{1,0},{2,3},{3,2},{4,5},{5,4},{6,7},{7,6},{8,9},{9,8},{10,11... | collective-permute-start | bytes 7077896 | tf_op jit(solution)/shard_map/ppermute | solution.py:622
  245.0 52.1 %collective-permute-start.28 = (bf16[2,8,48,1536]{3,2,1,0:T(8,128)(2,1)}, bf16[2,8,48,1536]{3,2,1,0:T(8,128)(2,1)}, u32[]{:S(2)}, u32[]{:S(2)}) collective-permute-start(bf16[2,8,48,1536]{3,2,1,0:T(8,128)(2,1)} %get-tuple-element.63), channel_id=1, source_target_pairs={{0,1},{1,0},{2,3},{3,2},{4,5},{5,4},{6,7},{7,6},{8,9},{9,8},{10,11... | collective-permute-start | bytes 7077896 | tf_op jit(solution)/shard_map/ppermute | solution.py:622
  248.3 44.2 %collective-permute-start.36 = (bf16[2,4,48,1536]{3,2,1,0:T(8,128)(2,1)}, bf16[2,4,48,1536]{3,2,1,0:T(8,128)(2,1)}, u32[]{:S(2)}, u32[]{:S(2)}) collective-permute-start(bf16[2,4,48,1536]{3,2,1,0:T(8,128)(2,1)} %fusion.1), channel_id=1, source_target_pairs={{0,2},{1,3},{2,0},{3,1},{4,6},{5,7},{6,4},{7,5},{8,10},{9,11},{10,... | collective-permute-start | bytes 3538952 | tf_op jit(solution)/shard_map/ppermute | solution.py:622
  250.2 26.5 %collective-permute-start.52 = (f32[4,768]{1,0:T(4,128)S(1)}, f32[4,768]{1,0:T(4,128)S(1)}, u32[]{:S(2)}, u32[]{:S(2)}) collective-permute-start(f32[4,768]{1,0:T(4,128)S(1)} %add.277), channel_id=1, source_target_pairs={{0,2},{1,3},{2,0},{3,1},{4,6},{5,7},{6,4},{7,5},{8,10},{9,11},{10,... | collective-permute-start | bytes 36872 | tf_op jit(solution)/shard_map/ppermute | solution.py:622
  296.4 16.3 %collective-permute-start.37 = (bf16[4,48,1536]{2,1,0:T(8,128)(2,1)S(1)}, bf16[4,48,1536]{2,1,0:T(8,128)(2,1)S(1)}, u32[]{:S(2)}, u32[]{:S(2)}) collective-permute-start(bf16[4,48,1536]{2,1,0:T(8,128)(2,1)S(1)} %fusion.4), channel_id=1, source_target_pairs={{0,16},{16,0},{1,17},{17,1},{2,18},{18,2},{3,19},{19,3},{4,20},{20... | collective-permute-start | bytes 1769480 | tf_op jit(solution)/shard_map/ppermute | solution.py:616
  300.1 37.9 %collective-permute-start.43 = (bf16[4,2,48,1536]{3,2,0,1:T(8,128)(2,1)S(1)}, bf16[4,2,48,1536]{3,2,0,1:T(8,128)(2,1)S(1)}, u32[]{:S(2)}, u32[]{:S(2)}) collective-permute-start(bf16[4,2,48,1536]{3,2,0,1:T(8,128)(2,1)S(1)} %fusion.2), channel_id=1, source_target_pairs={{0,16},{16,0},{1,17},{17,1},{2,18},{18,2},{3,19},{19,3},{4,20},{20... | collective-permute-start | bytes 3538952 | tf_op jit(solution)/shard_map/ppermute | solution.py:616
  312.9 11.7 %collective-permute-start.38 = (bf16[48,1536]{1,0:T(8,128)(2,1)S(1)}, bf16[48,1536]{1,0:T(8,128)(2,1)S(1)}, u32[]{:S(2)}, u32[]{:S(2)}) collective-permute-start(bf16[48,1536]{1,0:T(8,128)(2,1)S(1)} %get-tuple-element.82), channel_id=1, source_target_pairs={{0,4},{1,5},{2,6},{3,7},{4,8},{5,9},{6,10},{7,11},{8,12},{9,13},{1... | collective-permute-start | bytes 442376 | tf_op jit(solution)/shard_map/ppermute | solution.py:631
  313.5 18.7 %collective-permute-start.39 = (bf16[48,1536]{1,0:T(8,128)(2,1)S(1)}, bf16[48,1536]{1,0:T(8,128)(2,1)S(1)}, u32[]{:S(2)}, u32[]{:S(2)}) collective-permute-start(bf16[48,1536]{1,0:T(8,128)(2,1)S(1)} %get-tuple-element.84), channel_id=1, source_target_pairs={{0,8},{1,9},{2,10},{3,11},{4,12},{5,13},{6,14},{7,15},{8,0},{9,1},... | collective-permute-start | bytes 442376 | tf_op jit(solution)/shard_map/ppermute | solution.py:631
  316.7 15.4 %collective-permute-start.40 = (bf16[48,1536]{1,0:T(8,128)(2,1)S(1)}, bf16[48,1536]{1,0:T(8,128)(2,1)S(1)}, u32[]{:S(2)}, u32[]{:S(2)}) collective-permute-start(bf16[48,1536]{1,0:T(8,128)(2,1)S(1)} %get-tuple-element.83), channel_id=1, source_target_pairs={{0,12},{1,13},{2,14},{3,15},{4,0},{5,1},{6,2},{7,3},{8,4},{9,5},{1... | collective-permute-start | bytes 442376 | tf_op jit(solution)/shard_map/ppermute | solution.py:631
  317.3 44.2 %collective-permute-start.29 = (bf16[4,2,48,1536]{3,2,0,1:T(8,128)(2,1)S(1)}, bf16[4,2,48,1536]{3,2,0,1:T(8,128)(2,1)S(1)}, u32[]{:S(2)}, u32[]{:S(2)}) collective-permute-start(bf16[4,2,48,1536]{3,2,0,1:T(8,128)(2,1)S(1)} %fusion), channel_id=1, source_target_pairs={{0,16},{16,0},{1,17},{17,1},{2,18},{18,2},{3,19},{19,3},{4,20},{20... | collective-permute-start | bytes 3538952 | tf_op jit(solution)/shard_map/ppermute | solution.py:616
  332.3 30.8 %collective-permute-start.41 = (bf16[48,1536]{1,0:T(8,128)(2,1)S(1)}, bf16[48,1536]{1,0:T(8,128)(2,1)S(1)}, u32[]{:S(2)}, u32[]{:S(2)}) collective-permute-start(bf16[48,1536]{1,0:T(8,128)(2,1)S(1)} %fusion.14), channel_id=1, source_target_pairs={{0,16},{16,0},{1,17},{17,1},{2,18},{18,2},{3,19},{19,3},{4,20},{20... | collective-permute-start | bytes 442376 | tf_op jit(solution)/shard_map/ppermute | solution.py:616
  338.5 38.2 %collective-permute-start.44 = (bf16[4,48,1536]{2,1,0:T(8,128)(2,1)S(1)}, bf16[4,48,1536]{2,1,0:T(8,128)(2,1)S(1)}, u32[]{:S(2)}, u32[]{:S(2)}) collective-permute-start(bf16[4,48,1536]{2,1,0:T(8,128)(2,1)S(1)} %fusion.5), channel_id=1, source_target_pairs={{0,2},{1,3},{2,0},{3,1},{4,6},{5,7},{6,4},{7,5},{8,10},{9,11},{10,... | collective-permute-start | bytes 1769480 | tf_op jit(solution)/shard_map/ppermute | solution.py:622
  362.0 10.6 %collective-permute-start.30 = (bf16[4,48,1536]{2,1,0:T(8,128)(2,1)S(1)}, bf16[4,48,1536]{2,1,0:T(8,128)(2,1)S(1)}, u32[]{:S(2)}, u32[]{:S(2)}) collective-permute-start(bf16[4,48,1536]{2,1,0:T(8,128)(2,1)S(1)} %fusion.3), channel_id=1, source_target_pairs={{0,2},{1,3},{2,0},{3,1},{4,6},{5,7},{6,4},{7,5},{8,10},{9,11},{10,... | collective-permute-start | bytes 1769480 | tf_op jit(solution)/shard_map/ppermute | solution.py:622
  373.6 15.6 %collective-permute-start.32 = (bf16[48,1536]{1,0:T(8,128)(2,1)S(1)}, bf16[48,1536]{1,0:T(8,128)(2,1)S(1)}, u32[]{:S(2)}, u32[]{:S(2)}) collective-permute-start(bf16[48,1536]{1,0:T(8,128)(2,1)S(1)} %get-tuple-element.87), channel_id=1, source_target_pairs={{0,8},{1,9},{2,10},{3,11},{4,12},{5,13},{6,14},{7,15},{8,0},{9,1},... | collective-permute-start | bytes 442376 | tf_op jit(solution)/shard_map/ppermute | solution.py:631
  375.3 13.9 %collective-permute-start.33 = (bf16[48,1536]{1,0:T(8,128)(2,1)S(1)}, bf16[48,1536]{1,0:T(8,128)(2,1)S(1)}, u32[]{:S(2)}, u32[]{:S(2)}) collective-permute-start(bf16[48,1536]{1,0:T(8,128)(2,1)S(1)} %get-tuple-element.86), channel_id=1, source_target_pairs={{0,12},{1,13},{2,14},{3,15},{4,0},{5,1},{6,2},{7,3},{8,4},{9,5},{1... | collective-permute-start | bytes 442376 | tf_op jit(solution)/shard_map/ppermute | solution.py:631
  376.9 12.9 %collective-permute-start.45 = (bf16[48,1536]{1,0:T(8,128)(2,1)S(1)}, bf16[48,1536]{1,0:T(8,128)(2,1)S(1)}, u32[]{:S(2)}, u32[]{:S(2)}) collective-permute-start(bf16[48,1536]{1,0:T(8,128)(2,1)S(1)} %get-tuple-element.79), channel_id=1, source_target_pairs={{0,4},{1,5},{2,6},{3,7},{4,8},{5,9},{6,10},{7,11},{8,12},{9,13},{1... | collective-permute-start | bytes 442376 | tf_op jit(solution)/shard_map/ppermute | solution.py:631
  377.6 17.3 %collective-permute-start.46 = (bf16[48,1536]{1,0:T(8,128)(2,1)S(1)}, bf16[48,1536]{1,0:T(8,128)(2,1)S(1)}, u32[]{:S(2)}, u32[]{:S(2)}) collective-permute-start(bf16[48,1536]{1,0:T(8,128)(2,1)S(1)} %get-tuple-element.81), channel_id=1, source_target_pairs={{0,8},{1,9},{2,10},{3,11},{4,12},{5,13},{6,14},{7,15},{8,0},{9,1},... | collective-permute-start | bytes 442376 | tf_op jit(solution)/shard_map/ppermute | solution.py:631
  381.4 13.5 %collective-permute-start.47 = (bf16[48,1536]{1,0:T(8,128)(2,1)S(1)}, bf16[48,1536]{1,0:T(8,128)(2,1)S(1)}, u32[]{:S(2)}, u32[]{:S(2)}) collective-permute-start(bf16[48,1536]{1,0:T(8,128)(2,1)S(1)} %get-tuple-element.80), channel_id=1, source_target_pairs={{0,12},{1,13},{2,14},{3,15},{4,0},{5,1},{6,2},{7,3},{8,4},{9,5},{1... | collective-permute-start | bytes 442376 | tf_op jit(solution)/shard_map/ppermute | solution.py:631
  (61 other events, 492.3 us)
Sparse Core Ops, SparseCore 0:
  10.9 115.2 all-gather.2
  278.4 82.2 reduce-scatter.1
